TPU v7x, 32 devices: a whole 2x2x4 slice. The times are simulated.
32 devices in a mesh: expert: 8 (over z, y), head: 4 (over x, core).
Axes of the slice: x: 2, y: 2, z: 4, core: 2. Of those that a mesh axis runs over, the one named last changes fastest.
Arguments:
- block_input: bfloat16 [25216, 384], P(('expert', 'head')), may hold values from -6 to 6
- out_cotangent: bfloat16 [25216, 384], P(('expert', 'head')), may hold values from -6 to 6
- route_ids: int32 [25216, 2], P(('expert', 'head')), may hold values from 0 to 7, all different within a row; in each aligned block of 788 rows (0 to 787, 788 to 1575, ...) at most 590 rows name the same one
- capacity: int32 [8], replicated, may hold values from 148 to 295, as said below
- qkv_weight: float32 [384, 1152], P('head'), may hold values from -0.375 to 0.375
- qkv_first: float32 [384, 1152], P('head'), may hold values from -56 to 56
- qkv_second: float32 [384, 1152], P('head'), may hold values from 6.304 to 25.216
- proj_weight: float32 [384, 384], P('head'), may hold values from -1.25 to 1.25
- proj_first: float32 [384, 384], P('head'), may hold values from -28 to 28
- proj_second: float32 [384, 384], P('head'), may hold values from 1.576 to 6.304
- router_weight: float32 [384, 8], P('head'), may hold values from -0.25 to 0.25
- router_first: float32 [384, 8], P('head'), may hold values from -224 to 224
- router_second: float32 [384, 8], P('head'), may hold values from 100.864 to 403.456
- norm_params: float32 [384, 4], P('head'), may hold values from -2 to 2.5
- norm_first: float32 [384, 4], P('head'), may hold values from -56 to 56
- norm_second: float32 [384, 4], P('head'), may hold values from 6.304 to 25.216
- expert_up: float32 [8, 384, 1536], P('expert', None, 'head'), may hold values from -0.3125 to 0.3125
- up_first: float32 [8, 384, 1536], P('expert', None, 'head'), may hold values from -8 to 8
- up_second: float32 [8, 384, 1536], P('expert', None, 'head'), may hold values from 0.14184 to 0.56736
- expert_down: float32 [8, 384, 1536], P('expert', None, 'head'), may hold values from -0.15309311 to 0.15309311
- down_first: float32 [8, 384, 1536], P('expert', None, 'head'), may hold values from -16 to 16
- down_second: float32 [8, 384, 1536], P('expert', None, 'head'), may hold values from 0.56736 to 2.26944
Outputs:
- block_output: bfloat16 [25216, 384], P(('expert', 'head'))
- input_grad: bfloat16 [25216, 384], P(('expert', 'head'))
- qkv_new: float32 [384, 1152], P('head')
- qkv_copy: bfloat16 [384, 1152], P('head')
- qkv_first_new: float32 [384, 1152], P('head')
- qkv_second_new: float32 [384, 1152], P('head')
- proj_new: float32 [384, 384], P('head')
- proj_copy: bfloat16 [384, 384], P('head')
- proj_first_new: float32 [384, 384], P('head')
- proj_second_new: float32 [384, 384], P('head')
- router_new: float32 [384, 8], P('head')
- router_copy: bfloat16 [384, 8], P('head')
- router_first_new: float32 [384, 8], P('head')
- router_second_new: float32 [384, 8], P('head')
- norm_new: float32 [384, 4], P('head')
- norm_copy: bfloat16 [384, 4], P('head')
- norm_first_new: float32 [384, 4], P('head')
- norm_second_new: float32 [384, 4], P('head')
- up_new: float32 [8, 384, 1536], P('expert', None, 'head')
- up_copy: bfloat16 [8, 384, 1536], P('expert', None, 'head')
- up_first_new: float32 [8, 384, 1536], P('expert', None, 'head')
- up_second_new: float32 [8, 384, 1536], P('expert', None, 'head')
- down_new: float32 [8, 384, 1536], P('expert', None, 'head')
- down_copy: bfloat16 [8, 384, 1536], P('expert', None, 'head')
- down_first_new: float32 [8, 384, 1536], P('expert', None, 'head')
- down_second_new: float32 [8, 384, 1536], P('expert', None, 'head')
- dense_norms: float32 [7, 2], replicated
- expert_norms: float32 [8, 4], P('expert')
Inputs may be any that keep to these rules, and one draw needn't show every extreme that they name: `route_ids`: A token's two experts differ; in the 788 rows of one device no expert is named more than 2 * 295 times. One expert's capacity is exactly 295.
All inputs are finite; a program needn't handle non-finite values.
Results may differ from a plain program's by a relative error of at most 0.015.
The roundings to bfloat16 on the way count: a program that leaves them out, or rounds other values in their place, can miss the bound.
Values may be sent and summed in bfloat16 or wider, within the bound.
A program may use at most 192 MiB of HBM per device.

v0:
```python
import jax
import jax.numpy as jnp
from jax import lax
from jax.sharding import PartitionSpec as P

HEADS = 6
SEQ = 197
STEP = 5


beta_one = 0.9
beta_two = 0.999
adam_eps = 1e-06
decay_rate = 0.01
learn_rate = 0.4
norm_eps = 1e-06


def layer_norm(values, gain, shift):
    center = values - jnp.mean(values, axis=-1, keepdims=True)
    scale = lax.rsqrt(jnp.mean(center * center, axis=-1, keepdims=True) + norm_eps)
    return center * scale * gain + shift


def gelu_exact(values):
    return jax.nn.gelu(values, approximate=False)


def contract(left, right, left_dim, right_dim):
    return lax.dot_general(
        left, right, (((left_dim,), (right_dim,)), ((), ())), preferred_element_type=jnp.float32
    )


def squares(values):
    return jnp.sum(values * values)


def adam_terms(weight, grad, first, second):
    new_first = beta_one * first + (1.0 - beta_one) * grad
    new_second = beta_two * second + (1.0 - beta_two) * grad * grad
    corr_one = 1.0 - beta_one**STEP
    corr_two = 1.0 - beta_two**STEP
    update = (
        new_first / corr_one / (jnp.sqrt(new_second / corr_two) + adam_eps) + decay_rate * weight
    )
    return (new_first, new_second, update)


def routing(route_ids, capacity, experts, capsize):
    count = route_ids.shape[0]
    picks = route_ids[:, :, None] == jnp.arange(experts, dtype=jnp.int32)[None, None, :]
    order = jnp.transpose(picks, (1, 0, 2)).reshape(2 * count, experts).astype(jnp.int32)
    before = jnp.cumsum(order, axis=0) - order
    slot = jnp.sum(before * order, axis=1).reshape(2, count).T
    limit = jnp.sum(jnp.where(picks, capacity[None, None, :], 0), axis=2)
    kept = slot < limit
    position = jnp.where(kept, route_ids * capsize + slot, experts * capsize)
    return (picks, kept, position)


def forward(tokens, dense, expert_pair, picks, kept, position, capsize):
    qkv_w, proj_w, router_w, norm_w = dense
    up_w, down_w = expert_pair
    count, width = tokens.shape
    experts = router_w.shape[1]
    head_size = width // HEADS
    scale = head_size ** (-0.5)
    images = count // SEQ
    norm_f = norm_w.astype(jnp.float32)
    whole = tokens.astype(jnp.float32)
    first = layer_norm(whole, norm_f[:, 0], norm_f[:, 1]).astype(jnp.bfloat16)
    triple = jnp.dot(first, qkv_w, preferred_element_type=jnp.float32).astype(jnp.bfloat16)
    triple = triple.reshape(images, SEQ, 3, HEADS, head_size)
    query, key, value = (triple[:, :, 0], triple[:, :, 1], triple[:, :, 2])
    scores = jnp.einsum("isnd,itnd->inst", query, key, preferred_element_type=jnp.float32) * scale
    top = jnp.max(scores, axis=-1, keepdims=True)
    expo = jnp.exp(scores - top)
    summed = jnp.sum(expo, axis=-1, keepdims=True)
    logsum = top + jnp.log(summed)
    weights = (expo / summed).astype(jnp.bfloat16)
    mixed = jnp.einsum("inst,itnd->isnd", weights, value, preferred_element_type=jnp.float32)
    mixed = mixed.astype(jnp.bfloat16).reshape(count, width)
    resid = whole + jnp.dot(mixed, proj_w, preferred_element_type=jnp.float32)
    second = layer_norm(resid, norm_f[:, 2], norm_f[:, 3]).astype(jnp.bfloat16)
    logits = jnp.dot(second, router_w, preferred_element_type=jnp.float32)
    chosen = jnp.sum(jnp.where(picks, logits[:, None, :], 0.0), axis=2)
    gates = jax.nn.softmax(chosen, axis=-1)
    weighted = gates * kept.astype(jnp.float32)
    spread = jnp.broadcast_to(second[:, None, :], (count, 2, width)).reshape(2 * count, width)
    outgoing = (
        jnp.zeros((experts * capsize, width), jnp.bfloat16)
        .at[position.reshape(-1)]
        .set(spread, mode="drop")
    )
    rows = lax.all_to_all(
        outgoing.reshape(experts, capsize, width), "expert", split_axis=0, concat_axis=0, tiled=True
    )
    flat = rows.reshape(-1, width)
    pre = jnp.dot(flat, up_w, preferred_element_type=jnp.float32)
    hidden = gelu_exact(pre).astype(jnp.bfloat16)
    result = contract(hidden, down_w, 1, 1).astype(jnp.bfloat16)
    back = lax.all_to_all(
        result.reshape(rows.shape), "expert", split_axis=0, concat_axis=0, tiled=True
    )
    back, arrived, pre = (back, rows, pre.reshape(rows.shape[0], rows.shape[1], pre.shape[1]))
    returned = back.reshape(experts * capsize, width)[
        jnp.minimum(position, experts * capsize - 1)
    ].astype(jnp.float32)
    output = resid + jnp.sum(weighted[:, :, None] * returned, axis=1)
    return {
        "output": output,
        "first": first,
        "query": query,
        "key": key,
        "value": value,
        "logsum": logsum,
        "mixed": mixed,
        "resid": resid,
        "second": second,
        "gates": gates,
        "returned": returned,
        "arrived": arrived,
        "pre": pre,
    }


def local(
    block_input,
    out_cotangent,
    route_ids,
    capacity,
    qkv_weight,
    qkv_first,
    qkv_second,
    proj_weight,
    proj_first,
    proj_second,
    router_weight,
    router_first,
    router_second,
    norm_params,
    norm_first,
    norm_second,
    expert_up,
    up_first,
    up_second,
    expert_down,
    down_first,
    down_second,
):
    count, width = block_input.shape
    experts = router_weight.shape[1]
    capsize = max(2, 3 * count // lax.axis_size("expert"))
    dense = (
        lax.all_gather(qkv_weight.astype(jnp.bfloat16), "head", axis=0, tiled=True),
        lax.all_gather(proj_weight.astype(jnp.bfloat16), "head", axis=0, tiled=True),
        lax.all_gather(router_weight.astype(jnp.bfloat16), "head", axis=0, tiled=True),
        lax.all_gather(norm_params.astype(jnp.bfloat16), "head", axis=0, tiled=True),
    )
    expert_pair = (
        lax.all_gather(expert_up[0].astype(jnp.bfloat16), "head", axis=1, tiled=True),
        lax.all_gather(expert_down[0].astype(jnp.bfloat16), "head", axis=1, tiled=True),
    )
    picks, kept, position = routing(route_ids, capacity, experts, capsize)
    state = forward(block_input, dense, expert_pair, picks, kept, position, capsize)
    block_output = state["output"].astype(jnp.bfloat16)
    again = lax.optimization_barrier((block_input, state["output"]))[0]
    state = forward(again, dense, expert_pair, picks, kept, position, capsize)
    qkv_w, proj_w, router_w, norm_w = dense
    up_w, down_w = expert_pair
    norm_f = norm_w.astype(jnp.float32)
    head_size = width // HEADS
    scale = head_size ** (-0.5)
    images = count // SEQ
    dout = out_cotangent.astype(jnp.float32)
    keptf = kept.astype(jnp.float32)
    gates = state["gates"]
    weighted = gates * keptf
    dweighted = jnp.sum(dout[:, None, :] * state["returned"], axis=2) * keptf
    dchosen = gates * (dweighted - jnp.sum(gates * dweighted, axis=1, keepdims=True))
    dlogits = jnp.sum(jnp.where(picks, dchosen[:, :, None], 0.0), axis=1).astype(jnp.bfloat16)
    danswer = (
        (weighted[:, :, None] * dout[:, None, :]).astype(jnp.bfloat16).reshape(2 * count, width)
    )
    outgoing = (
        jnp.zeros((experts * capsize, width), jnp.bfloat16)
        .at[position.reshape(-1)]
        .set(danswer, mode="drop")
    )
    arrived = lax.all_to_all(
        outgoing.reshape(experts, capsize, width), "expert", split_axis=0, concat_axis=0, tiled=True
    )
    dflat = arrived.reshape(-1, width)
    rows = state["arrived"].reshape(-1, width)
    pre = state["pre"].reshape(rows.shape[0], -1)
    hidden, gelu_back = jax.vjp(gelu_exact, pre)
    hidden16 = hidden.astype(jnp.bfloat16)
    dpre = gelu_back(jnp.dot(dflat, down_w, preferred_element_type=jnp.float32))[0].astype(
        jnp.bfloat16
    )
    grad_down = contract(dflat, hidden16, 0, 0)
    grad_up = contract(rows, dpre, 0, 0)
    drows = contract(dpre, up_w, 1, 1).astype(jnp.bfloat16)
    back = lax.all_to_all(
        drows.reshape(arrived.shape), "expert", split_axis=0, concat_axis=0, tiled=True
    )
    taken = back.reshape(experts * capsize, width)[
        jnp.minimum(position, experts * capsize - 1)
    ].astype(jnp.float32)
    dsecond = jnp.sum(taken * keptf[:, :, None], axis=1) + contract(dlogits, router_w, 1, 1)
    grad_router = contract(state["second"], dlogits, 0, 0)
    _, second_back = jax.vjp(layer_norm, state["resid"], norm_f[:, 2], norm_f[:, 3])
    dresid, dgain_two, dshift_two = second_back(dsecond)
    dresid = dresid + dout
    dattn = dresid.astype(jnp.bfloat16)
    grad_proj = contract(state["mixed"], dattn, 0, 0)
    dmixed = (
        contract(dattn, proj_w, 1, 1).astype(jnp.bfloat16).reshape(images, SEQ, HEADS, head_size)
    )
    query, key, value = (state["query"], state["key"], state["value"])
    scores = jnp.einsum("isnd,itnd->inst", query, key, preferred_element_type=jnp.float32) * scale
    probs = jnp.exp(scores - state["logsum"])
    dvalue = jnp.einsum(
        "inst,isnd->itnd", probs.astype(jnp.bfloat16), dmixed, preferred_element_type=jnp.float32
    )
    dprobs = jnp.einsum("isnd,itnd->inst", dmixed, value, preferred_element_type=jnp.float32)
    dscores = (probs * (dprobs - jnp.sum(dprobs * probs, axis=-1, keepdims=True))).astype(
        jnp.bfloat16
    )
    dquery = jnp.einsum("inst,itnd->isnd", dscores, key, preferred_element_type=jnp.float32) * scale
    dkey = jnp.einsum("inst,isnd->itnd", dscores, query, preferred_element_type=jnp.float32) * scale
    dtriple = (
        jnp.stack([dquery, dkey, dvalue], axis=2).astype(jnp.bfloat16).reshape(count, 3 * width)
    )
    grad_qkv = contract(state["first"], dtriple, 0, 0)
    dfirst = contract(dtriple, qkv_w, 1, 1)
    _, first_back = jax.vjp(layer_norm, block_input.astype(jnp.float32), norm_f[:, 0], norm_f[:, 1])
    dinput, dgain_one, dshift_one = first_back(dfirst)
    input_grad = (dinput + dresid).astype(jnp.bfloat16)
    grad_norm = jnp.stack([dgain_one, dshift_one, dgain_two, dshift_two], axis=1)
    summed = lax.psum((grad_qkv, grad_proj, grad_router, grad_norm), ("expert", "head"))
    rows_dev = qkv_weight.shape[0]
    start = lax.axis_index("head") * rows_dev
    shares = tuple((lax.dynamic_slice_in_dim(total, start, rows_dev, 0) for total in summed))
    expert_grads = (
        lax.psum_scatter(grad_up, "head", scatter_dimension=1, tiled=True),
        lax.psum_scatter(grad_down, "head", scatter_dimension=1, tiled=True),
    )
    qkv_m, qkv_v, qkv_r = adam_terms(qkv_weight, shares[0], qkv_first, qkv_second)
    proj_m, proj_v, proj_r = adam_terms(proj_weight, shares[1], proj_first, proj_second)
    router_m, router_v, router_r = adam_terms(router_weight, shares[2], router_first, router_second)
    norm_m, norm_v, norm_r = adam_terms(norm_params, shares[3], norm_first, norm_second)
    up_m, up_v, up_r = adam_terms(expert_up, expert_grads[0][None], up_first, up_second)
    down_m, down_v, down_r = adam_terms(expert_down, expert_grads[1][None], down_first, down_second)
    weight_col = jnp.concatenate(
        [
            jnp.stack([squares(qkv_weight), squares(proj_weight), squares(router_weight)]),
            jnp.sum(norm_params * norm_params, axis=0),
        ]
    )
    update_col = jnp.concatenate(
        [
            jnp.stack([squares(qkv_r), squares(proj_r), squares(router_r)]),
            jnp.sum(norm_r * norm_r, axis=0),
        ]
    )
    expert_sq = jnp.stack(
        [squares(expert_up), squares(up_r), squares(expert_down), squares(down_r)]
    )[None, :]
    totals = lax.psum((jnp.stack([weight_col, update_col], axis=1), expert_sq), "head")
    dense_norms = jnp.sqrt(totals[0])
    expert_norms = jnp.sqrt(totals[1])
    trust = dense_norms[:, 0] / dense_norms[:, 1]
    qkv_new = qkv_weight - learn_rate * trust[0] * qkv_r
    proj_new = proj_weight - learn_rate * trust[1] * proj_r
    router_new = router_weight - learn_rate * trust[2] * router_r
    norm_new = norm_params - learn_rate * trust[3:][None, :] * norm_r
    up_new = expert_up - learn_rate * (expert_norms[0, 0] / expert_norms[0, 1]) * up_r
    down_new = expert_down - learn_rate * (expert_norms[0, 2] / expert_norms[0, 3]) * down_r
    return (
        block_output,
        input_grad,
        qkv_new,
        qkv_new.astype(jnp.bfloat16),
        qkv_m,
        qkv_v,
        proj_new,
        proj_new.astype(jnp.bfloat16),
        proj_m,
        proj_v,
        router_new,
        router_new.astype(jnp.bfloat16),
        router_m,
        router_v,
        norm_new,
        norm_new.astype(jnp.bfloat16),
        norm_m,
        norm_v,
        up_new,
        up_new.astype(jnp.bfloat16),
        up_m,
        up_v,
        down_new,
        down_new.astype(jnp.bfloat16),
        down_m,
        down_v,
        dense_norms,
        expert_norms,
    )


def solution(mesh):
    return jax.shard_map(
        local,
        mesh=mesh,
        in_specs=(
            P(("expert", "head"), None),
            P(("expert", "head"), None),
            P(("expert", "head"), None),
            P(),
            P("head", None),
            P("head", None),
            P("head", None),
            P("head", None),
            P("head", None),
            P("head", None),
            P("head", None),
            P("head", None),
            P("head", None),
            P("head", None),
            P("head", None),
            P("head", None),
            P("expert", None, "head"),
            P("expert", None, "head"),
            P("expert", None, "head"),
            P("expert", None, "head"),
            P("expert", None, "head"),
            P("expert", None, "head"),
        ),
        out_specs=(
            P(("expert", "head"), None),
            P(("expert", "head"), None),
            P("head", None),
            P("head", None),
            P("head", None),
            P("head", None),
            P("head", None),
            P("head", None),
            P("head", None),
            P("head", None),
            P("head", None),
            P("head", None),
            P("head", None),
            P("head", None),
            P("head", None),
            P("head", None),
            P("head", None),
            P("head", None),
            P("expert", None, "head"),
            P("expert", None, "head"),
            P("expert", None, "head"),
            P("expert", None, "head"),
            P("expert", None, "head"),
            P("expert", None, "head"),
            P("expert", None, "head"),
            P("expert", None, "head"),
            P(),
            P("expert", None),
        ),
        check_vma=False,
    )
```

profile of v0, /device:TPU:0, one launch (start us, length us, event | category | flops | bytes accessed | tf_op | source)
XLA Modules:
  0.0 863.5 jit_solution(14394304904244088738)
XLA Ops:
  10.6 6.0 all-gather.2
  23.5 7.9 all_gather.20
  31.8 9.3 %all_gather.19 = bf16[384,1152]{1,0:T(8,128)(2,1)S(1)} all-gather(bf16[96,1152]{1,0:T(8,128)(2,1)S(1)} %convert_element_type.163), channel_id=1, replica_groups=mesh['expert'=8,'head'=4] {'head'}, dimensions={0}, use_global_device_ids=true | all-gather | bytes 1105920 | tf_op jit(solution)/shard_map/all_gather | solution.py:156
  71.6 11.3 %scatter_custom_fusion = bf16[2360,384]{1,0:T(8,128)(2,1)S(1)} fusion(s32[1576]{0:T(1024)S(1)} %fusion.105, bf16[1576,384]{1,0:T(8,128)(2,1)} %reshape.381, bf16[]{:T(256)} %constant.61.clone.1), kind=kCustom, calls=%fused_computation.128 | custom fusion | bytes 1812992 | tf_op jit(solution)/shard_map/scatter | solution.py:94
  92.0 40.9 %all-to-all-done = bf16[8,295,384]{2,1,0:T(8,128)(2,1)S(1)} async-done(((bf16[8,295,384]{2,1,0:T(8,128)(2,1)}), bf16[8,295,384]{2,1,0:T(8,128)(2,1)S(1)}, u32[]{:S(2)}, u32[]{:S(2)}) %all-to-all-start) | async-done | bytes 1812512 | tf_op jit(solution)/shard_map/all_to_all | solution.py:96
  134.7 37.0 %convolution_convert_fusion.2 = bf16[2360,384]{1,0:T(8,128)(2,1)S(1)} fusion(bf16[2360,384]{1,0:T(8,128)(2,1)} %reshape.337, bf16[1,384,1536]{2,1,0:T(8,128)(2,1)} %all-gather.9.cloned.1.call-done, bf16[1,384,1536]{2,1,0:T(8,128)(2,1)} %all-gather.7.cloned.1.call-done), kind=kOutput, calls=%fused_computation.55 | convolution fusion | flops 5804467200 | bytes 5984256 | tf_op jit(solution)/shard_map/dot_general | solution.py:30
  185.0 34.9 %all-to-all-done.1 = bf16[8,295,384]{2,1,0:T(8,128)(2,1)} async-done(((bf16[8,295,384]{2,1,0:T(8,128)(2,1)}), bf16[8,295,384]{2,1,0:T(8,128)(2,1)}, u32[]{:S(2)}, u32[]{:S(2)}) %all-to-all-start.1) | async-done | bytes 1812512 | tf_op jit(solution)/shard_map/all_to_all | solution.py:103
  221.9 5.9 gather_fusion
  267.2 11.8 %scatter_custom_fusion.1 = bf16[2360,384]{1,0:T(8,128)(2,1)} fusion(s32[1576]{0:T(1024)S(1)} %fusion.105, bf16[1576,384]{1,0:T(8,128)(2,1)S(1)} %reshape.389, bf16[]{:T(256)} %constant.61.clone.1), kind=kCustom, calls=%fused_computation.126 | custom fusion | bytes 1812482 | tf_op jit(solution)/shard_map/scatter | solution.py:94
  281.0 46.3 %all_to_all.30 = bf16[8,295,384]{2,1,0:T(8,128)(2,1)} all-to-all(bf16[8,295,384]{2,1,0:T(8,128)(2,1)S(1)} %reshape.343), channel_id=1, replica_groups=mesh['expert'=8,'head'=4] {'expert'}, dimensions={0} | all-to-all | bytes 3624960 | tf_op jit(solution)/shard_map/all_to_all | solution.py:96
  329.4 36.3 %multiply_convert_fusion = (bf16[2360,1536]{1,0:T(8,128)(2,1)S(1)}, f32[2360,1536]{1,0:T(8,128)}, f32[2360,1536]{1,0:T(8,128)}) fusion(bf16[2360,384]{1,0:T(8,128)(2,1)S(1)} %reshape.344, bf16[1,384,1536]{2,1,0:T(8,128)(2,1)} %all-gather.7.cloned.1.call-done), kind=kOutput, calls=%fused_computation.13 | convolution fusion | flops 3019591680 | bytes 39241728 | tf_op jit(solution)/shard_map/dot_general | solution.py:100
  386.6 33.8 %all-to-all-done.5 = bf16[8,295,384]{2,1,0:T(8,128)(2,1)} async-done(((bf16[8,295,384]{2,1,0:T(8,128)(2,1)}), bf16[8,295,384]{2,1,0:T(8,128)(2,1)}, u32[]{:S(2)}, u32[]{:S(2)}) %all-to-all-start.5) | async-done | bytes 1812512 | tf_op jit(solution)/shard_map/all_to_all | solution.py:103
  422.4 5.9 gather_fusion.2
  436.1 17.5 %scatter_custom_fusion.2 = bf16[2360,384]{1,0:T(8,128)(2,1)S(1)} fusion(s32[1576]{0:T(1024)S(1)} %fusion.105, f32[1576,384]{1,0:T(8,128)} %mul.620, f32[1576]{0:T(1024)S(1)} %mul.617, bf16[]{:T(256)} %constant.61.clone.1), kind=kCustom, calls=%fused_computation.116 | custom fusion | flops 1210368 | bytes 4241410 | tf_op jit(solution)/shard_map/scatter | solution.py:189
  455.5 46.7 %all_to_all.31 = bf16[8,295,384]{2,1,0:T(8,128)(2,1)} all-to-all(bf16[8,295,384]{2,1,0:T(8,128)(2,1)} %reshape.345), channel_id=1, replica_groups=mesh['expert'=8,'head'=4] {'expert'}, dimensions={0} | all-to-all | bytes 3624960 | tf_op jit(solution)/shard_map/all_to_all | solution.py:191
  504.2 16.8 %add_convert_fusion = bf16[2360,1536]{1,0:T(8,128)(2,1)} fusion(f32[2360,1536]{1,0:T(8,128)} %get-tuple-element.227, bf16[2360,384]{1,0:T(8,128)(2,1)S(1)} %reshape.346, f32[2360,1536]{1,0:T(8,128)} %get-tuple-element.257, bf16[1,384,1536]{2,1,0:T(8,128)(2,1)} %all-gather.9.cloned.1.call-done), kind=kOutput, calls=%fused_computation.14 | convolution fusion | flops 2834718720 | bytes 39241728 | tf_op jit(solution)/shard_map/dot_general | solution.py:199
  521.0 8.3 convolution_convert_fusion.1
  537.3 41.0 %all-to-all-done.4 = bf16[8,295,384]{2,1,0:T(8,128)(2,1)} async-done(((bf16[8,295,384]{2,1,0:T(8,128)(2,1)}), bf16[8,295,384]{2,1,0:T(8,128)(2,1)}, u32[]{:S(2)}, u32[]{:S(2)}) %all-to-all-start.4) | async-done | bytes 1812512 | tf_op jit(solution)/shard_map/all_to_all | solution.py:205
  626.9 8.3 fusion.176
  635.4 8.3 fusion.177
  650.4 37.3 %all-reduce.1 = (f32[384,4]{0,1:T(4,128)S(1)}, f32[384,8]{0,1:T(8,128)S(1)}) all-reduce(f32[384,4]{0,1:T(4,128)S(1)} %pad_maximum_fusion.1, f32[384,8]{0,1:T(8,128)S(1)} %fusion.178), channel_id=1, replica_groups=mesh['expert'=8,'head'=4] {'expert','head'}, use_global_device_ids=true, to_apply=%region_49.50 | all-reduce | flops 4608 | bytes 36864 | tf_op jit(solution)/shard_map/psum | solution.py:242
  691.8 68.9 %all-reduce.6.cloned.1.call-done = (f32[384,384]{1,0:T(8,128)}, f32[384,1152]{1,0:T(8,128)}) async-done(((f32[384,384]{1,0:T(8,128)}, f32[384,1152]{1,0:T(8,128)}), (f32[384,384]{1,0:T(8,128)}, f32[384,1152]{1,0:T(8,128)})) %all-reduce.6.cloned.1.call-update) | async-done | bytes 2359312 | tf_op jit(solution)/shard_map/psum | solution.py:242
  770.3 24.8 %reduce-scatter.3.cloned.1.call-done = f32[384,384]{1,0:T(8,128)} async-done(((f32[384,1536]{1,0:T(8,128)}), f32[384,384]{1,0:T(8,128)}) %reduce-scatter.3.cloned.1.call-update) | async-done | bytes 589840 | tf_op jit(solution)/shard_map/reduce_scatter | solution.py:247
  797.5 33.1 %reduce-scatter.5.cloned.1.call-done = f32[384,384]{1,0:T(8,128)} async-done(((f32[384,1536]{1,0:T(8,128)}), f32[384,384]{1,0:T(8,128)}) %reduce-scatter.5.cloned.1.call-update) | async-done | bytes 589840 | tf_op jit(solution)/shard_map/reduce_scatter | solution.py:248
  (355 shorter events, 245.3 us)
Async XLA Ops:
  7.2 127.5 %all-gather.7.cloned.1.call-start = ((), (), s32[]{:S(2)}) async-start(), calls=%async_computation.10 | async-start | bytes 1474560 | tf_op jit(solution)/shard_map/all_gather | solution.py:162
  16.7 221.5 %copy-start.62 = (f32[384]{0:T(512)}, f32[384]{0:T(512)S(1)}, u32[]{:S(2)}) copy-start(f32[384]{0:T(512)S(1)} %get-tuple-element.187) | copy-start | bytes 4612
  16.7 221.5 %copy-start.75 = (f32[384]{0:T(512)}, f32[384]{0:T(512)S(1)}, u32[]{:S(2)}) copy-start(f32[384]{0:T(512)S(1)} %get-tuple-element.186) | copy-start | bytes 4612
  16.7 245.2 %copy-start.51 = (f32[384]{0:T(512)}, f32[384]{0:T(512)S(1)}, u32[]{:S(2)}) copy-start(f32[384]{0:T(512)S(1)} %get-tuple-element.184) | copy-start | bytes 4612
  23.4 160.6 %copy-start.45 = (pred[788,2]{0,1:T(4,128)(4,1)}, pred[788,2]{0,1:T(4,128)(4,1)S(1)}, u32[]{:S(2)}) copy-start(pred[788,2]{0,1:T(4,128)(4,1)S(1)} %get-tuple-element.229) | copy-start | bytes 4732
  31.3 229.4 %copy-start.22 = (bf16[384,384]{1,0:T(8,128)(2,1)}, bf16[384,384]{1,0:T(8,128)(2,1)S(1)}, u32[]{:S(2)}) copy-start(bf16[384,384]{1,0:T(8,128)(2,1)S(1)} %all_gather.20) | copy-start | bytes 884740
  84.6 48.3 %all-to-all-start = ((bf16[8,295,384]{2,1,0:T(8,128)(2,1)}), bf16[8,295,384]{2,1,0:T(8,128)(2,1)S(1)}, u32[]{:S(2)}, u32[]{:S(2)}) async-start(bf16[8,295,384]{2,1,0:T(8,128)(2,1)} %reshape.336), calls=%async_computation | async-start | bytes 3637248 | tf_op jit(solution)/shard_map/all_to_all | solution.py:96
  90.1 44.6 %all-gather.9.cloned.1.call-start = ((), (), s32[]{:S(2)}) async-start(), calls=%async_computation.11 | async-start | bytes 1474560 | tf_op jit(solution)/shard_map/all_gather | solution.py:163
  173.5 46.4 %all-to-all-start.1 = ((bf16[8,295,384]{2,1,0:T(8,128)(2,1)}), bf16[8,295,384]{2,1,0:T(8,128)(2,1)}, u32[]{:S(2)}, u32[]{:S(2)}) async-start(bf16[8,295,384]{2,1,0:T(8,128)(2,1)} %reshape.338), calls=%async_computation.1 | async-start | bytes 3637248 | tf_op jit(solution)/shard_map/all_to_all | solution.py:103
  262.5 123.8 %copy-start.11 = (bf16[788,384]{1,0:T(8,128)(2,1)}, bf16[788,384]{1,0:T(8,128)(2,1)S(1)}, u32[]{:S(2)}) copy-start(bf16[788,384]{1,0:T(8,128)(2,1)S(1)} %add_convert_fusion.2) | copy-start | bytes 1815556
  374.3 46.1 %all-to-all-start.5 = ((bf16[8,295,384]{2,1,0:T(8,128)(2,1)}), bf16[8,295,384]{2,1,0:T(8,128)(2,1)}, u32[]{:S(2)}, u32[]{:S(2)}) async-start(bf16[8,295,384]{2,1,0:T(8,128)(2,1)} %reshape.349), calls=%async_computation.5 | async-start | bytes 3637248 | tf_op jit(solution)/shard_map/all_to_all | solution.py:103
  532.5 45.8 %all-to-all-start.4 = ((bf16[8,295,384]{2,1,0:T(8,128)(2,1)}), bf16[8,295,384]{2,1,0:T(8,128)(2,1)}, u32[]{:S(2)}, u32[]{:S(2)}) async-start(bf16[8,295,384]{2,1,0:T(8,128)(2,1)} %reshape.347), calls=%async_computation.4 | async-start | bytes 3637248 | tf_op jit(solution)/shard_map/all_to_all | solution.py:205
  537.0 223.6 %all-reduce.6.cloned.1.call-start = ((), (), s32[]{:S(2)}) async-start(), calls=%async_computation.12 | async-start | bytes 4718592 | tf_op jit(solution)/shard_map/psum | solution.py:242
  626.8 168.3 %reduce-scatter.3.cloned.1.call-start = ((), (), s32[]{:S(2)}) async-start(), calls=%async_computation.8 | async-start | bytes 2949120 | tf_op jit(solution)/shard_map/reduce_scatter | solution.py:247
  635.2 195.4 %reduce-scatter.5.cloned.1.call-start = ((), (), s32[]{:S(2)}) async-start(), calls=%async_computation.9 | async-start | bytes 2949120 | tf_op jit(solution)/shard_map/reduce_scatter | solution.py:248
  650.3 110.4 %copy-start.33 = (f32[96,384]{1,0:T(8,128)S(1)}, f32[96,384]{1,0:T(8,128)}, u32[]{:S(2)}) copy-start(f32[96,384]{1,0:T(8,128)} %param.29) | copy-start | bytes 442372
  689.1 160.4 %copy-start.67 = (f32[96,8]{0,1:T(8,128)}, f32[96,8]{0,1:T(8,128)S(1)}, u32[]{:S(2)}) copy-start(f32[96,8]{0,1:T(8,128)S(1)} %get-tuple-element.216) | copy-start | bytes 9220
  689.1 160.4 %copy-start.68 = (f32[96,8]{0,1:T(8,128)}, f32[96,8]{0,1:T(8,128)S(1)}, u32[]{:S(2)}) copy-start(f32[96,8]{0,1:T(8,128)S(1)} %get-tuple-element.217) | copy-start | bytes 9220
  689.1 74.0 %copy-start.25 = (f32[96,1152]{1,0:T(8,128)S(1)}, f32[96,1152]{1,0:T(8,128)}, u32[]{:S(2)}) copy-start(f32[96,1152]{1,0:T(8,128)} %param.26) | copy-start | bytes 1327108
  691.8 74.5 %copy-start.77 = (f32[4]{0:T(128)S(1)}, f32[4]{0:T(128)}, u32[]{:S(2)}) copy-start(f32[4]{0:T(128)} %get-tuple-element.244) | copy-start | bytes 52
  691.8 103.3 %copy-start.19 = (f32[1,384,384]{2,1,0:T(8,128)S(1)}, f32[1,384,384]{2,1,0:T(8,128)}, u32[]{:S(2)}) copy-start(f32[1,384,384]{2,1,0:T(8,128)} %param.38) | copy-start | bytes 1769476
  691.8 103.3 %copy-start.37 = (f32[1,384,384]{2,1,0:T(8,128)S(1)}, f32[1,384,384]{2,1,0:T(8,128)}, u32[]{:S(2)}) copy-start(f32[1,384,384]{2,1,0:T(8,128)} %param.39) | copy-start | bytes 1769476
  766.3 64.3 %copy-start.18 = (f32[1,384,384]{2,1,0:T(8,128)S(1)}, f32[1,384,384]{2,1,0:T(8,128)}, u32[]{:S(2)}) copy-start(f32[1,384,384]{2,1,0:T(8,128)} %param.41) | copy-start | bytes 1769476
  797.5 58.0 %copy-start.29 = (f32[1,384,384]{2,1,0:T(8,128)}, f32[1,384,384]{2,1,0:T(8,128)S(1)}, u32[]{:S(2)}) copy-start(f32[1,384,384]{2,1,0:T(8,128)S(1)} %get-tuple-element.209) | copy-start | bytes 1769476
  (69 other events, 772.0 us)
Sparse Core Ops, SparseCore 0:
  10.2 21.5 all-gather.6
  93.1 17.9 all-gather.8
  626.9 133.6 all-reduce.5
  763.2 31.8 reduce-scatter.2
  797.5 33.0 reduce-scatter.4
where the time goes:
time: 871 us; the launch traced here: 863 us
  waiting for transfers between devices  277 us (32%)
  blocking collectives  164 us (19%)
  matrix products  149 us (17%)
  local copies, waits for them, and re-layouts  148 us (17%)
  other arithmetic  85.1 us (10%)
  between operations  20.1 us (2%)
  starting transfers between devices  19.5 us (2%)
    dot_general x11, matrix products, contract(): lax.dot_general(left, right, (((left_dim,), (right_dim,)), ((), ())), pre...  77.7 us
    psum x1, waiting for transfers between devices, local(): lax.psum((grad_qkv, grad_proj, grad_router, grad_norm), ('expert', 'head'))  68.9 us
    all_to_all x2, waiting for transfers between devices, forward(): lax.all_to_all(result.reshape(rows.shape), 'expert', split_axis=0, concat...  68.6 us
    all_to_all x1, blocking collectives, local(): lax.all_to_all(outgoing.reshape(experts, capsize, width), 'expert', split...  46.7 us
    all_to_all x1, blocking collectives, forward(): lax.all_to_all(outgoing.reshape(experts, capsize, width), 'expert', split...  46.3 us
    all_to_all x1, waiting for transfers between devices, local(): lax.all_to_all(drows.reshape(arrived.shape), 'expert', split_axis=0, conc...  41 us
    all_to_all x1, waiting for transfers between devices, forward(): lax.all_to_all(outgoing.reshape(experts, capsize, width), 'expert', split...  40.9 us
    psum x1, blocking collectives, local(): lax.psum((grad_qkv, grad_proj, grad_router, grad_norm), ('expert', 'head'))  37.3 us
  transfers between devices with their start and end apart: 9, of which 7 were waited for; matrix products, arithmetic and copies ran while one was open for 12% of the time, Pallas kernels for 0%

commit v1 on v0

v1 whole, which is shorter than its diff:
```python
import functools
import jax
import jax.numpy as jnp
from jax import lax
from jax.experimental import pallas as pl
from jax.experimental.pallas import tpu as pltpu
from jax.sharding import PartitionSpec as P

HEADS = 6
SEQ = 197
STEP = 5
ROWS = 208
KEYS = 256
LANES = 128

beta_one = 0.9
beta_two = 0.999
adam_eps = 1e-06
decay_rate = 0.01
learn_rate = 0.4
norm_eps = 1e-06

F32 = jnp.float32
BF16 = jnp.bfloat16
VMEM = pl.BlockSpec(memory_space=pltpu.VMEM)


def nn(left, right):
    return lax.dot_general(left, right, (((1,), (0,)), ((), ())), preferred_element_type=F32)


def nt(left, right):
    return lax.dot_general(left, right, (((1,), (1,)), ((), ())), preferred_element_type=F32)


def tn(left, right):
    return lax.dot_general(left, right, (((0,), (0,)), ((), ())), preferred_element_type=F32)


def params(mib=56, **more):
    return pltpu.CompilerParams(vmem_limit_bytes=mib * 2**20, **more)


def ceil_to(value, step):
    return -(-value // step) * step


def normed(values):
    center = values - jnp.mean(values, axis=1, keepdims=True)
    scale = lax.rsqrt(jnp.mean(center * center, axis=1, keepdims=True) + norm_eps)
    return center * scale, scale


def lane_index(rows, lanes):
    return lax.broadcasted_iota(jnp.int32, (rows, lanes), 1)


def attend_body(images, experts, slots, refs):
    (
        tokens, dout, routes, limits, norms, qkv, proj, router,
        first, triple, logsum, mixed, resid, second, pos, gates, sent,
        whole, dpad, wide, picked, weighted,
    ) = refs
    count = images * SEQ
    total = images * ROWS
    width = tokens.shape[1]
    head_size = width // HEADS
    scale = head_size ** (-0.5)
    wide[0:count, :] = tokens[...].astype(F32)
    whole[...] = jnp.zeros_like(whole)
    for i in range(images):
        whole[i * ROWS : i * ROWS + SEQ, :] = wide[i * SEQ : (i + 1) * SEQ, :]
    wide[0:count, :] = dout[...].astype(F32)
    for i in range(images):
        dpad[i * ROWS : (i + 1) * ROWS, :] = jnp.concatenate(
            [wide[i * SEQ : (i + 1) * SEQ, :], jnp.zeros((ROWS - SEQ, width), F32)], axis=0
        ).astype(BF16)
    ids = routes[...].astype(F32)
    picked[...] = jnp.full(picked.shape, -1.0, F32)
    for i in range(images):
        picked[i * ROWS : i * ROWS + SEQ, 0:2] = ids[i * SEQ : (i + 1) * SEQ, :]
    lanes = lane_index(total, LANES).astype(F32)
    one = jnp.where(lanes == picked[:, 0:1], 1.0, 0.0)
    two = jnp.where(lanes == picked[:, 1:2], 1.0, 0.0)
    firsts = jnp.sum(one, axis=0, keepdims=True)
    both = jnp.concatenate([one.astype(BF16), two.astype(BF16)], axis=1)
    gain_one, shift_one = norms[0:1, :], norms[1:2, :]
    gain_two, shift_two = norms[2:3, :], norms[3:4, :]
    triple[total:, :] = jnp.zeros((triple.shape[0] - total, triple.shape[1]), BF16)

    def project(i, carry):
        rows = pl.ds(pl.multiple_of(i * ROWS, 16), ROWS)
        ready = (normed(whole[rows, :])[0] * gain_one + shift_one).astype(BF16)
        first[rows, :] = ready
        triple[rows, :] = nn(ready, qkv[...]).astype(BF16)
        return carry

    lax.fori_loop(0, images, project, 0)
    low = lane_index(1, LANES) < head_size
    real = lane_index(1, KEYS) < SEQ
    spot = lane_index(1, LANES)

    def image(i, carry):
        start = pl.multiple_of(i * ROWS, 16)
        rows = pl.ds(start, ROWS)
        keys = pl.ds(start, KEYS)
        sums = jnp.zeros((ROWS, LANES), F32)
        for pair in range(HEADS // 2):
            at = pair * 2 * head_size
            query = triple[rows, at : at + LANES]
            key = triple[keys, width + at : width + at + LANES]
            value = triple[keys, 2 * width + at : 2 * width + at + LANES]
            blend = jnp.zeros((ROWS, LANES), F32)
            for side in range(2):
                mine = low if side == 0 else jnp.logical_not(low)
                scores = nt(query, jnp.where(mine, key, 0.0).astype(BF16)) * scale
                scores = jnp.where(real, scores, -1e30)
                top = jnp.max(scores, axis=1, keepdims=True)
                expo = jnp.exp(scores - top)
                summed = jnp.sum(expo, axis=1, keepdims=True)
                sums = jnp.where(spot == pair * 2 + side, top + jnp.log(summed), sums)
                weights = (expo * (1.0 / summed)).astype(BF16)
                blend = blend + nn(weights, jnp.where(mine, value, 0.0).astype(BF16))
            mixed[rows, at : at + LANES] = blend.astype(BF16)
        logsum[rows, :] = sums
        after = whole[rows, :] + nn(mixed[rows, :], proj[...])
        resid[rows, :] = after
        ready = (normed(after)[0] * gain_two + shift_two).astype(BF16)
        second[rows, :] = ready
        logits = nn(ready, router[...])
        lane = lane_index(ROWS, LANES).astype(F32)
        choose = picked[rows, :]
        hot_one = lane == choose[:, 0:1]
        hot_two = lane == choose[:, 1:2]
        level_one = jnp.sum(jnp.where(hot_one, logits, 0.0), axis=1, keepdims=True)
        level_two = jnp.sum(jnp.where(hot_two, logits, 0.0), axis=1, keepdims=True)
        top = jnp.maximum(level_one, level_two)
        expo_one = jnp.exp(level_one - top)
        expo_two = jnp.exp(level_two - top)
        summed = expo_one + expo_two
        gate = jnp.where(hot_one, expo_one / summed, jnp.where(hot_two, expo_two / summed, 0.0))
        gates[rows, :] = gate
        column = lax.broadcasted_iota(jnp.int32, (ROWS, total), 1)
        row = lax.broadcasted_iota(jnp.int32, (ROWS, total), 0) + start
        earlier = nn(jnp.where(column < row, 1.0, 0.0).astype(BF16), both)
        slot = jnp.where(hot_one, earlier[:, :LANES], earlier[:, LANES:] + firsts)
        kept = jnp.logical_and(jnp.logical_or(hot_one, hot_two), slot < limits[...])
        pos[rows, :] = jnp.where(kept, slot, -1.0)
        weighted[rows, :] = jnp.where(kept, gate, 0.0)
        return carry

    lax.fori_loop(0, images, image, 0)
    across = jnp.transpose(pos[...])
    weights_across = jnp.transpose(weighted[...])
    picked_rows = across.shape[0]
    pos_rows, weight_rows = across, weights_across
    for e in range(experts):
        slot = lax.broadcasted_iota(jnp.int32, (slots, total), 0).astype(F32)
        hit = slot == pos_rows[e : e + 1, :]
        share = jnp.sum(jnp.where(hit, weight_rows[e : e + 1, :], 0.0), axis=1, keepdims=True)
        place = jnp.where(hit, 1.0, 0.0).astype(BF16)
        sent[e, :, 0:width] = nn(place, second[...]).astype(BF16)
        sent[e, :, width:] = (nn(place, dpad[...]) * share).astype(BF16)


def attend(tokens, dout, routes, limits, norms, qkv, proj, router, experts, slots):
    count, width = tokens.shape
    images = count // SEQ
    total = images * ROWS
    shape = jax.ShapeDtypeStruct
    return pl.pallas_call(
        lambda *refs: attend_body(images, experts, slots, refs),
        out_shape=(
            shape((total, width), BF16),
            shape((total + KEYS - ROWS, 3 * width), BF16),
            shape((total, LANES), F32),
            shape((total, width), BF16),
            shape((total, width), F32),
            shape((total, width), BF16),
            shape((total, LANES), F32),
            shape((total, LANES), F32),
            shape((experts, slots, 2 * width), BF16),
        ),
        in_specs=[VMEM] * 8,
        out_specs=tuple([VMEM] * 9),
        scratch_shapes=[
            pltpu.VMEM((total, width), F32),
            pltpu.VMEM((total, width), BF16),
            pltpu.VMEM((ceil_to(count, 8), width), F32),
            pltpu.VMEM((total, LANES), F32),
            pltpu.VMEM((total, LANES), F32),
        ],
        compiler_params=params(),
        name="attend",
    )(tokens, dout, routes, limits, norms, qkv, proj, router)


def gelu_pair(pre):
    half = 0.5 + 0.5 * lax.erf(pre * 0.7071067811865476)
    slope = half + pre * (jnp.exp(pre * pre * -0.5) * 0.3989422804014327)
    return pre * half, slope


def chunk_rows(total):
    size = 320
    while total % size:
        size -= 16
    return size


def expert_body(rows, chunk, tile, refs):
    (arrived, up, down, back, grad_up, grad_down, hidden_all, dpre_all) = refs
    width = up.shape[0]
    hidden_size = up.shape[1]

    def block(b, carry):
        at = pl.ds(pl.multiple_of(b * chunk, 16), chunk)
        x = arrived[at, 0:width]
        da = arrived[at, width:]
        answer = jnp.zeros((chunk, width), F32)
        drow = jnp.zeros((chunk, width), F32)
        for j in range(hidden_size // tile):
            cols = slice(j * tile, (j + 1) * tile)
            hidden, slope = gelu_pair(nn(x, up[:, cols]))
            hidden = hidden.astype(BF16)
            dpre = (nn(da, down[:, cols]) * slope).astype(BF16)
            hidden_all[at, cols] = hidden
            dpre_all[at, cols] = dpre
            answer = answer + nt(hidden, down[:, cols])
            drow = drow + nt(dpre, up[:, cols])
        back[at, 0:width] = answer.astype(BF16)
        back[at, width:] = drow.astype(BF16)
        return carry

    lax.fori_loop(0, rows // chunk, block, 0)

    def grads(j, carry):
        cols = pl.ds(pl.multiple_of(j * 256, 256), 256)
        grad_up[:, cols] = tn(arrived[:, 0:width], dpre_all[:, cols])
        grad_down[:, cols] = tn(arrived[:, width:], hidden_all[:, cols])
        return carry

    lax.fori_loop(0, hidden_size // 256, grads, 0)


def expert(arrived, up, down):
    rows = arrived.shape[0]
    width, hidden = up.shape
    chunk = chunk_rows(rows)
    shape = jax.ShapeDtypeStruct
    return pl.pallas_call(
        lambda *refs: expert_body(rows, chunk, 512, refs),
        out_shape=(
            shape((rows, 2 * width), BF16),
            shape((width, hidden), F32),
            shape((width, hidden), F32),
        ),
        in_specs=[VMEM] * 3,
        out_specs=(VMEM, VMEM, VMEM),
        scratch_shapes=[pltpu.VMEM((rows, hidden), BF16), pltpu.VMEM((rows, hidden), BF16)],
        compiler_params=params(),
        name="expert",
    )(arrived, up, down)


def norm_back(grad, values, gain):
    xhat, scale = normed(values)
    dgain = jnp.sum(grad * xhat, axis=0, keepdims=True)
    dshift = jnp.sum(grad, axis=0, keepdims=True)
    inner = grad * gain
    mean_one = jnp.mean(inner, axis=1, keepdims=True)
    mean_two = jnp.mean(inner * xhat, axis=1, keepdims=True)
    return (inner - mean_one - xhat * mean_two) * scale, dgain, dshift


def back_body(images, experts, slots, refs):
    (
        tokens, dout, norms, qkv, proj, router,
        first, triple, logsum, mixed, resid, second, pos, gates, back,
        output, input_grad, grads,
        wide, whole, dpad, outs, dwe, drow, dtriple, dres, dkeys, dvals, dmix, small,
    ) = refs
    count = images * SEQ
    total = images * ROWS
    width = tokens.shape[1]
    head_size = width // HEADS
    scale = head_size ** (-0.5)
    gain_one, gain_two = norms[0:1, :], norms[2:3, :]
    wide[0:count, :] = tokens[...].astype(F32)
    whole[...] = jnp.zeros_like(whole)
    for i in range(images):
        whole[i * ROWS : i * ROWS + SEQ, :] = wide[i * SEQ : (i + 1) * SEQ, :]
    wide[0:count, :] = dout[...].astype(F32)
    dpad[...] = jnp.zeros_like(dpad)
    for i in range(images):
        dpad[i * ROWS : i * ROWS + SEQ, :] = wide[i * SEQ : (i + 1) * SEQ, :]
    outs[...] = resid[...]
    dwe[...] = jnp.zeros_like(dwe)
    drow[...] = jnp.zeros_like(drow)
    lane = lane_index(ROWS, LANES)
    slot = lane_index(ROWS, slots).astype(F32)

    def combine(i, carry):
        rows = pl.ds(pl.multiple_of(i * ROWS, 16), ROWS)
        dhere = dpad[rows, :]
        out = resid[rows, :]
        dws = jnp.zeros((ROWS, LANES), F32)
        dr = jnp.zeros((ROWS, width), F32)
        place_at = pos[rows, :]
        gate = gates[rows, :]
        for e in range(experts):
            at = place_at[:, e : e + 1]
            place = jnp.where(slot == at, 1.0, 0.0).astype(BF16)
            both = nn(place, back[e])
            answer = both[:, 0:width]
            share = jnp.where(at >= 0.0, gate[:, e : e + 1], 0.0)
            out = out + share * answer
            dws = jnp.where(lane == e, jnp.sum(dhere * answer, axis=1, keepdims=True), dws)
            dr = dr + both[:, width:]
        outs[rows, :] = out
        dchosen = gate * (dws - jnp.sum(gate * dws, axis=1, keepdims=True))
        dlogits = dchosen.astype(BF16)
        dwe[rows, :] = dlogits
        drow[rows, :] = dr + nt(dlogits, router[...])
        return carry

    lax.fori_loop(0, images, combine, 0)
    for i in range(images):
        wide[i * SEQ : (i + 1) * SEQ, :] = outs[i * ROWS : i * ROWS + SEQ, :]
    output[...] = wide[0:count, :].astype(BF16)
    small[...] = jnp.zeros_like(small)

    def second_norm(i, carry):
        rows = pl.ds(pl.multiple_of(i * ROWS, 16), ROWS)
        dx, dgain, dshift = norm_back(drow[rows, :], resid[rows, :], gain_two)
        dx = dx + dpad[rows, :]
        small[2:3, :] += dgain
        small[3:4, :] += dshift
        dres[rows, :] = dx
        dattn = dx.astype(BF16)
        drow[rows, :] = dx
        dmix[rows, :] = nt(dattn, proj[...]).astype(BF16)
        return carry

    lax.fori_loop(0, images, second_norm, 0)
    low = lane_index(1, LANES) < head_size
    real = lane_index(1, KEYS) < SEQ
    zero = jnp.zeros((), BF16)

    def image(i, carry):
        start = pl.multiple_of(i * ROWS, 16)
        rows = pl.ds(start, ROWS)
        keys = pl.ds(start, KEYS)
        sums = logsum[rows, :]
        for pair in range(HEADS // 2):
            at = pair * 2 * head_size
            query = triple[rows, at : at + LANES]
            key = triple[keys, width + at : width + at + LANES]
            value = triple[keys, 2 * width + at : 2 * width + at + LANES]
            dm = dmix[rows, at : at + LANES]
            dq = jnp.zeros((ROWS, LANES), F32)
            dk = jnp.zeros((KEYS, LANES), F32)
            dv = jnp.zeros((KEYS, LANES), F32)
            for side in range(2):
                mine = low if side == 0 else jnp.logical_not(low)
                head = pair * 2 + side
                key_mine = jnp.where(mine, key, zero)
                scores = nt(query, key_mine) * scale
                probs = jnp.where(real, jnp.exp(scores - sums[:, head : head + 1]), 0.0)
                dprobs = nt(jnp.where(mine, dm, zero), value)
                inner = jnp.sum(dprobs * probs, axis=1, keepdims=True)
                dscores = (probs * (dprobs - inner)).astype(BF16)
                dv = dv + tn(probs.astype(BF16), jnp.where(mine, dm, zero))
                dq = dq + nn(dscores, key_mine)
                dk = dk + tn(dscores, jnp.where(mine, query, zero))
            dtriple[rows, at : at + LANES] = (dq * scale).astype(BF16)
            dtriple[rows, width + at : width + at + LANES] = (dk * scale)[:ROWS].astype(BF16)
            dtriple[rows, 2 * width + at : 2 * width + at + LANES] = dv[:ROWS].astype(BF16)
        dfirst = nt(dtriple[rows, :], qkv[...])
        dx, dgain, dshift = norm_back(dfirst, whole[rows, :], gain_one)
        small[0:1, :] += dgain
        small[1:2, :] += dshift
        dres[rows, :] += dx
        return carry

    lax.fori_loop(0, images, image, 0)
    for i in range(images):
        wide[i * SEQ : (i + 1) * SEQ, :] = dres[i * ROWS : i * ROWS + SEQ, :]
    input_grad[...] = wide[0:count, :].astype(BF16)
    grads[:, 0 : 3 * width] = tn(first[...], dtriple[...])
    grads[:, 3 * width : 4 * width] = tn(mixed[...], drow[...].astype(BF16))
    tail = tn(second[...], dwe[...])
    columns = jnp.transpose(jnp.concatenate([small[...], jnp.zeros((LANES - 8, width), F32)], axis=0))
    shifted = pltpu.roll(columns, experts, 1)
    grads[:, 4 * width :] = jnp.where(lane_index(width, LANES) < experts, tail, shifted)


def backward(tokens, dout, norms, qkv, proj, router, saved, back, experts, slots):
    count, width = tokens.shape
    images = count // SEQ
    total = images * ROWS
    shape = jax.ShapeDtypeStruct
    return pl.pallas_call(
        lambda *refs: back_body(images, experts, slots, refs),
        out_shape=(
            shape((count, width), BF16),
            shape((count, width), BF16),
            shape((width, 4 * width + LANES), F32),
        ),
        in_specs=[VMEM] * 15,
        out_specs=(VMEM, VMEM, VMEM),
        scratch_shapes=[
            pltpu.VMEM((ceil_to(count, 8), width), F32),
            pltpu.VMEM((total, width), F32),
            pltpu.VMEM((total, width), F32),
            pltpu.VMEM((total, width), F32),
            pltpu.VMEM((total, LANES), BF16),
            pltpu.VMEM((total, width), F32),
            pltpu.VMEM((total, 3 * width), BF16),
            pltpu.VMEM((total, width), F32),
            pltpu.VMEM((8, LANES), BF16),
            pltpu.VMEM((8, LANES), BF16),
            pltpu.VMEM((total, width), BF16),
            pltpu.VMEM((8, width), F32),
        ],
        compiler_params=params(),
        name="backward",
    )(tokens, dout, norms, qkv, proj, router, *saved, back)


def squares(values):
    return jnp.sum(values * values)


def adam_terms(weight, grad, first, second):
    new_first = beta_one * first + (1.0 - beta_one) * grad
    new_second = beta_two * second + (1.0 - beta_two) * grad * grad
    corr_one = 1.0 - beta_one**STEP
    corr_two = 1.0 - beta_two**STEP
    update = (
        new_first / corr_one / (jnp.sqrt(new_second / corr_two) + adam_eps) + decay_rate * weight
    )
    return (new_first, new_second, update)


def local(
    block_input, out_cotangent, route_ids, capacity,
    qkv_weight, qkv_first, qkv_second,
    proj_weight, proj_first, proj_second,
    router_weight, router_first, router_second,
    norm_params, norm_first, norm_second,
    expert_up, up_first, up_second,
    expert_down, down_first, down_second,
):
    count, width = block_input.shape
    experts = router_weight.shape[1]
    capsize = max(2, 3 * count // lax.axis_size("expert"))
    slots = ceil_to(capsize, 16)
    rows_dev = qkv_weight.shape[0]
    dense = jnp.concatenate(
        [qkv_weight, proj_weight, router_weight, norm_params,
         jnp.zeros((rows_dev, LANES - experts - 4), F32)], axis=1
    ).astype(BF16)
    dense = lax.all_gather(dense, "head", axis=0, tiled=True)
    up_w = lax.all_gather(expert_up[0].astype(BF16), "head", axis=1, tiled=True)
    down_w = lax.all_gather(expert_down[0].astype(BF16), "head", axis=1, tiled=True)
    qkv = dense[:, 0 : 3 * width]
    proj = dense[:, 3 * width : 4 * width]
    tail = dense[:, 4 * width :]
    router = jnp.where(jnp.arange(LANES)[None, :] < experts, tail, 0)
    norms = jnp.pad(tail[:, experts : experts + 4].astype(F32).T, ((0, 4), (0, 0)))
    limits = jnp.pad(capacity.astype(F32), (0, LANES - experts))[None, :]
    *saved, sent = attend(
        block_input, out_cotangent, route_ids, limits, norms, qkv, proj, router, experts, slots
    )
    arrived = lax.all_to_all(sent, "expert", split_axis=0, concat_axis=0, tiled=True)
    back, grad_up, grad_down = expert(arrived.reshape(experts * slots, 2 * width), up_w, down_w)
    back = lax.all_to_all(
        back.reshape(experts, slots, 2 * width), "expert", split_axis=0, concat_axis=0, tiled=True
    )
    block_output, input_grad, grads = backward(
        block_input, out_cotangent, norms, qkv, proj, router, saved, back, experts, slots
    )
    summed = lax.psum_scatter(grads, "head", scatter_dimension=0, tiled=True)
    summed = lax.psum(summed, "expert")
    shares = (
        summed[:, 0 : 3 * width],
        summed[:, 3 * width : 4 * width],
        summed[:, 4 * width : 4 * width + experts],
        summed[:, 4 * width + experts : 4 * width + experts + 4],
    )
    expert_grads = (
        lax.psum_scatter(grad_up, "head", scatter_dimension=1, tiled=True),
        lax.psum_scatter(grad_down, "head", scatter_dimension=1, tiled=True),
    )
    qkv_m, qkv_v, qkv_r = adam_terms(qkv_weight, shares[0], qkv_first, qkv_second)
    proj_m, proj_v, proj_r = adam_terms(proj_weight, shares[1], proj_first, proj_second)
    router_m, router_v, router_r = adam_terms(router_weight, shares[2], router_first, router_second)
    norm_m, norm_v, norm_r = adam_terms(norm_params, shares[3], norm_first, norm_second)
    up_m, up_v, up_r = adam_terms(expert_up, expert_grads[0][None], up_first, up_second)
    down_m, down_v, down_r = adam_terms(expert_down, expert_grads[1][None], down_first, down_second)
    weight_col = jnp.concatenate(
        [
            jnp.stack([squares(qkv_weight), squares(proj_weight), squares(router_weight)]),
            jnp.sum(norm_params * norm_params, axis=0),
        ]
    )
    update_col = jnp.concatenate(
        [
            jnp.stack([squares(qkv_r), squares(proj_r), squares(router_r)]),
            jnp.sum(norm_r * norm_r, axis=0),
        ]
    )
    expert_sq = jnp.stack(
        [squares(expert_up), squares(up_r), squares(expert_down), squares(down_r)]
    )[None, :]
    totals = lax.psum((jnp.stack([weight_col, update_col], axis=1), expert_sq), "head")
    dense_norms = jnp.sqrt(totals[0])
    expert_norms = jnp.sqrt(totals[1])
    trust = dense_norms[:, 0] / dense_norms[:, 1]
    qkv_new = qkv_weight - learn_rate * trust[0] * qkv_r
    proj_new = proj_weight - learn_rate * trust[1] * proj_r
    router_new = router_weight - learn_rate * trust[2] * router_r
    norm_new = norm_params - learn_rate * trust[3:][None, :] * norm_r
    up_new = expert_up - learn_rate * (expert_norms[0, 0] / expert_norms[0, 1]) * up_r
    down_new = expert_down - learn_rate * (expert_norms[0, 2] / expert_norms[0, 3]) * down_r
    return (
        block_output, input_grad,
        qkv_new, qkv_new.astype(BF16), qkv_m, qkv_v,
        proj_new, proj_new.astype(BF16), proj_m, proj_v,
        router_new, router_new.astype(BF16), router_m, router_v,
        norm_new, norm_new.astype(BF16), norm_m, norm_v,
        up_new, up_new.astype(BF16), up_m, up_v,
        down_new, down_new.astype(BF16), down_m, down_v,
        dense_norms, expert_norms,
    )


def solution(mesh):
    tokens, dense, pair = P(("expert", "head"), None), P("head", None), P("expert", None, "head")
    return jax.shard_map(
        local,
        mesh=mesh,
        in_specs=(tokens,) * 3 + (P(),) + (dense,) * 12 + (pair,) * 6,
        out_specs=(tokens,) * 2 + (dense,) * 16 + (pair,) * 8 + (P(), P("expert", None)),
        check_vma=False,
    )
```

time: 871 us -> 541 us (0.62)
  matrix products: 149 us -> 0 us
  local copies, waits for them, and re-layouts: 148 us -> 31 us
  Pallas kernels: 0 us -> 80.9 us
  blocking collectives: 164 us -> 94.2 us
  other arithmetic: 85.1 us -> 40.6 us
  starting transfers between devices: 19.5 us -> 5.94 us
  waiting for transfers between devices: 277 us -> 267 us
    dot_general x27 -> x0, matrix products: 149 us -> none  [the longest x11 77.7 us: contract(): lax.dot_general(left, right, (((left_dim,), (right_dim,)), ((), ())), pre...]
    all_to_all x4 -> x1, waiting for transfers between devices: 151 us -> 43.3 us  [local(): lax.all_to_all(sent, 'expert', split_axis=0, concat_axis=0, tiled=True)]
    pallas_call x0 -> x3, Pallas kernels: none -> 80.9 us  [the longest x1 31.2 us: expert(): pl.pallas_call(lambda *refs: expert_body(rows, chunk, 512, refs), out_sha...]
    all_gather x2 -> x3, waiting for transfers between devices: 0.01 us -> 57.5 us  [the longest x1 19.6 us: local(): lax.all_gather(expert_down[0].astype(BF16), 'head', axis=1, tiled=True)]
    reshape x22 -> x0, local copies, waits for them, and re-layouts: 44 us -> none  [the longest x2 9.59 us: forward(): triple = triple.reshape(images, SEQ, 3, HEADS, head_size)]
    psum x1 -> x0, blocking collectives: 37.3 us -> none  [local(): lax.psum((grad_qkv, grad_proj, grad_router, grad_norm), ('expert', 'head'))]
    all_gather x4 -> x0, blocking collectives: 28.3 us -> none  [the longest x1 9.25 us: local(): lax.all_gather(qkv_weight.astype(jnp.bfloat16), 'head', axis=0, tiled=True)]
    reduce_scatter x0 -> x1, waiting for transfers between devices: none -> 25.6 us  [local(): summed = lax.psum_scatter(grads, 'head', scatter_dimension=0, tiled=True)]
  transfers between devices with their start and end apart: 9 -> 8, of which waited for: 7 -> 8; matrix products, arithmetic and copies ran while one was open for 12% -> 3% of each run, Pallas kernels for 0% -> 0%
where the time goes in v1:
time: 541 us; the launch traced here: 539 us
  waiting for transfers between devices  267 us (49%)
  blocking collectives  94.2 us (17%)
  Pallas kernels  80.9 us (15%)
  other arithmetic  40.6 us (8%)
  local copies, waits for them, and re-layouts  31 us (6%)
  between operations  18.9 us (3%)
  starting transfers between devices  5.94 us (1%)
    all_to_all x1, blocking collectives, local(): lax.all_to_all(back.reshape(experts, slots, 2 * width), 'expert', split_a...  88 us
    psum x1, waiting for transfers between devices, local(): summed = lax.psum(summed, 'expert')  70.7 us
    all_to_all x1, waiting for transfers between devices, local(): lax.all_to_all(sent, 'expert', split_axis=0, concat_axis=0, tiled=True)  43.3 us
    reduce_scatter x1, waiting for transfers between devices, local(): lax.psum_scatter(grad_down, 'head', scatter_dimension=1, tiled=True)  35.6 us
    reduce_scatter x1, waiting for transfers between devices, local(): lax.psum_scatter(grad_up, 'head', scatter_dimension=1, tiled=True)  33.3 us
    pallas_call x1, Pallas kernels, expert(): pl.pallas_call(lambda *refs: expert_body(rows, chunk, 512, refs), out_sha...  31.2 us
    pallas_call x1, Pallas kernels, backward(): pl.pallas_call(lambda *refs: back_body(images, experts, slots, refs), out...  28.6 us
    reduce_scatter x1, waiting for transfers between devices, local(): summed = lax.psum_scatter(grads, 'head', scatter_dimension=0, tiled=True)  25.6 us
  transfers between devices with their start and end apart: 8, of which 8 were waited for; matrix products, arithmetic and copies ran while one was open for 3% of the time, Pallas kernels for 0%

profile of v1, /device:TPU:0, one launch (start us, length us, event | category | flops | bytes accessed | tf_op | source)
XLA Modules:
  0.0 538.8 jit_solution(12356544519628612289)
XLA Ops:
  15.2 18.7 %all-gather.6.cloned.1.call-done = bf16[384,1664]{1,0:T(8,128)(2,1)} async-done(((bf16[96,1664]{1,0:T(8,128)(2,1)}), bf16[384,1664]{1,0:T(8,128)(2,1)}) %all-gather.6.cloned.1.call-update) | async-done | bytes 1277968 | tf_op jit(solution)/shard_map/all_gather | solution.py:464
  35.7 2.2 slice.78.refs_5_.refs_3_
  41.1 21.2 %attend.1 = (bf16[832,384]{1,0:T(8,128)(2,1)}, bf16[880,1152]{1,0:T(8,128)(2,1)}, f32[832,128]{1,0:T(8,128)}, bf16[832,384]{1,0:T(8,128)(2,1)}, f32[832,384]{1,0...) custom-call(bf16[788,384]{1,0:T(8,128)(2,1)} %refs_0_.3, ...), custom_call_target="tpu_custom_call" | custom-call | tf_op jit(solution)/shard_map/attend/pallas_call | solution.py:171
  62.3 5.7 %all-to-all-start = ((bf16[8,304,768]{2,1,0:T(8,128)(2,1)}), bf16[8,304,768]{2,1,0:T(8,128)(2,1)}, u32[]{:S(2)}, u32[]{:S(2)}) async-start(bf16[8,304,768]{2,1,0:T(8,128)(2,1)} %get-tuple-element.51), calls=%async_computation | async-start | bytes 7471104 | tf_op jit(solution)/shard_map/all_to_all | solution.py:476
  69.7 19.2 %all-gather.8.cloned.1.call-done = bf16[1,384,1536]{2,1,0:T(8,128)(2,1)} async-done(((bf16[1,384,384]{2,1,0:T(8,128)(2,1)}), bf16[1,384,1536]{2,1,0:T(8,128)(2,1)}) %all-gather.8.cloned.1.call-update) | async-done | bytes 1179664 | tf_op jit(solution)/shard_map/all_gather | solution.py:465
  88.9 19.6 %all-gather.10.cloned.1.call-done = bf16[1,384,1536]{2,1,0:T(8,128)(2,1)} async-done(((bf16[1,384,384]{2,1,0:T(8,128)(2,1)}), bf16[1,384,1536]{2,1,0:T(8,128)(2,1)}) %all-gather.10.cloned.1.call-update) | async-done | bytes 1179664 | tf_op jit(solution)/shard_map/all_gather | solution.py:466
  108.5 43.3 %all-to-all-done = bf16[8,304,768]{2,1,0:T(8,128)(2,1)} async-done(((bf16[8,304,768]{2,1,0:T(8,128)(2,1)}), bf16[8,304,768]{2,1,0:T(8,128)(2,1)}, u32[]{:S(2)}, u32[]{:S(2)}) %all-to-all-start) | async-done | bytes 3735584 | tf_op jit(solution)/shard_map/all_to_all | solution.py:476
  151.8 31.2 %expert.1 = (bf16[2432,768]{1,0:T(8,128)(2,1)}, f32[384,1536]{1,0:T(8,128)}, f32[384,1536]{1,0:T(8,128)}) custom-call(bf16[2432,768]{1,0:T(8,128)(2,1)} %bitcast.2.refs_0_, bf16[384,1536]{1,0:T(8,128)(2,1)} %bitcast.48, bf16[384,1536]{1,0:T(8,128)(2,1)} %bitcast.49), custom_call_target="tpu_custom_call" | custom-call | tf_op jit(solution)/shard_map/expert/pallas_call | solution.py:251
  183.0 88.0 %all_to_all.10.refs_14_ = bf16[8,304,768]{2,1,0:T(8,128)(2,1)} all-to-all(bf16[8,304,768]{2,1,0:T(8,128)(2,1)} %bitcast.47), channel_id=1, replica_groups=mesh['expert'=8,'head'=4] {'expert'}, dimensions={0} | all-to-all | bytes 7471104 | tf_op jit(solution)/shard_map/all_to_all | solution.py:478
  271.0 28.6 %backward.1 = (bf16[788,384]{1,0:T(8,128)(2,1)}, bf16[788,384]{1,0:T(8,128)(2,1)}, f32[384,1664]{1,0:T(8,128)}) custom-call(bf16[788,384]{1,0:T(8,128)(2,1)} %refs_0_.3, bf16[788,384]{1,0:T(8,128)(2,1)} %refs_1_.3, f32[8,384]{1,0:T(8,128)} %copy.87.refs_4_.refs_2_, bf16[384,1152]{1,0:T(8,128)(2,1)} %slice.78.refs_5_.refs_3_, ...), custom_call_target="tpu_custom_call" | custom-call | tf_op jit(solution)/shard_map/backward/pallas_call | solution.py:403
  305.9 25.6 %reduce-scatter.4.cloned.1.call-done = f32[96,1664]{1,0:T(8,128)} async-done(((f32[384,1664]{1,0:T(8,128)}), f32[96,1664]{1,0:T(8,128)}) %reduce-scatter.4.cloned.1.call-update) | async-done | bytes 638992 | tf_op jit(solution)/shard_map/reduce_scatter | solution.py:484
  331.5 35.6 %reduce-scatter.8.cloned.1.call-done = f32[384,384]{1,0:T(8,128)} async-done(((f32[384,1536]{1,0:T(8,128)}), f32[384,384]{1,0:T(8,128)}) %reduce-scatter.8.cloned.1.call-update) | async-done | bytes 589840 | tf_op jit(solution)/shard_map/reduce_scatter | solution.py:494
  367.1 2.2 multiply_reduce_fusion.1
  369.3 33.3 %reduce-scatter.6.cloned.1.call-done = f32[384,384]{1,0:T(8,128)} async-done(((f32[384,1536]{1,0:T(8,128)}), f32[384,384]{1,0:T(8,128)}) %reduce-scatter.6.cloned.1.call-update) | async-done | bytes 589840 | tf_op jit(solution)/shard_map/reduce_scatter | solution.py:493
  402.6 3.3 multiply_reduce_fusion.3
  405.9 2.7 maximum_bitcast_fusion.2
  409.3 70.7 %all-reduce.5.cloned.1.call-done = f32[96,1664]{1,0:T(8,128)} async-done(((f32[96,1664]{1,0:T(8,128)}), f32[96,1664]{1,0:T(8,128)}) %all-reduce.5.cloned.1.call-update) | async-done | bytes 638992 | tf_op jit(solution)/shard_map/psum | solution.py:485
  483.5 3.2 multiply_reduce_fusion.5
  486.7 2.3 multiply_reduce_fusion.7
  489.0 2.1 multiply_reduce_fusion.8
  491.1 4.6 maximum_bitcast_fusion
  495.7 6.2 %all-reduce.2 = (f32[7,2]{0,1:T(2,128)}, f32[1,4]{0,1:T(4,128)S(1)}) all-reduce(f32[7,2]{0,1:T(2,128)S(1)} %pad_maximum_fusion, f32[1,4]{0,1:T(4,128)S(1)} %copy-done.17), channel_id=1, replica_groups=mesh['expert'=8,'head'=4] {'head'}, use_global_device_ids=true, to_apply=%region_10.11 | all-reduce | flops 18 | bytes 144 | tf_op jit(solution)/shard_map/psum | solution.py:517
  525.4 2.2 fusion.13
  527.7 1.8 fusion.12
  (119 shorter events, 46.4 us)
Async XLA Ops:
  7.2 7.5 %copy-start.23 = (s32[8]{0:T(128)S(1)}, s32[8]{0:T(128)}, u32[]{:S(2)}) copy-start(s32[8]{0:T(128)} %param.25) | copy-start | bytes 100
  7.2 26.7 %all-gather.6.cloned.1.call-start = ((), (), s32[]{:S(2)}) async-start(), calls=%async_computation.5 | async-start | bytes 1597440 | tf_op jit(solution)/shard_map/all_gather | solution.py:464
  62.3 5.7 %copy-start = (f32[1,384,384]{2,1,0:T(8,128)S(1)}, f32[1,384,384]{2,1,0:T(8,128)}, u32[]{:S(2)}) copy-start(f32[1,384,384]{2,1,0:T(8,128)} %param.38) | copy-start | bytes 1769476
  62.3 6.5 %copy-start.1 = (f32[1,384,384]{2,1,0:T(8,128)S(1)}, f32[1,384,384]{2,1,0:T(8,128)}, u32[]{:S(2)}) copy-start(f32[1,384,384]{2,1,0:T(8,128)} %param.41) | copy-start | bytes 1769476
  62.3 89.5 %all-to-all-start = ((bf16[8,304,768]{2,1,0:T(8,128)(2,1)}), bf16[8,304,768]{2,1,0:T(8,128)(2,1)}, u32[]{:S(2)}, u32[]{:S(2)}) async-start(bf16[8,304,768]{2,1,0:T(8,128)(2,1)} %get-tuple-element.51), calls=%async_computation | async-start | bytes 7471104 | tf_op jit(solution)/shard_map/all_to_all | solution.py:476
  68.0 20.9 %all-gather.8.cloned.1.call-start = ((), (), s32[]{:S(2)}) async-start(), calls=%async_computation.10 | async-start | bytes 1474560 | tf_op jit(solution)/shard_map/all_gather | solution.py:465
  68.8 39.7 %all-gather.10.cloned.1.call-start = ((), (), s32[]{:S(2)}) async-start(), calls=%async_computation.11 | async-start | bytes 1474560 | tf_op jit(solution)/shard_map/all_gather | solution.py:466
  69.6 261.8 %reduce-scatter.4.cloned.1.call-start = ((), (), s32[]{:S(2)}) async-start(), calls=%async_computation.6 | async-start | bytes 3194880 | tf_op jit(solution)/shard_map/reduce_scatter | solution.py:484
  299.6 67.5 %reduce-scatter.8.cloned.1.call-start = ((), (), s32[]{:S(2)}) async-start(), calls=%async_computation.9 | async-start | bytes 2949120 | tf_op jit(solution)/shard_map/reduce_scatter | solution.py:494
  299.7 67.4 %copy-start.8 = (f32[1,384,384]{2,1,0:T(8,128)S(1)}, f32[1,384,384]{2,1,0:T(8,128)}, u32[]{:S(2)}) copy-start(f32[1,384,384]{2,1,0:T(8,128)} %param.42) | copy-start | bytes 1769476
  299.7 67.4 %copy-start.9 = (f32[1,384,384]{2,1,0:T(8,128)S(1)}, f32[1,384,384]{2,1,0:T(8,128)}, u32[]{:S(2)}) copy-start(f32[1,384,384]{2,1,0:T(8,128)} %param.43) | copy-start | bytes 1769476
  300.2 102.4 %reduce-scatter.6.cloned.1.call-start = ((), (), s32[]{:S(2)}) async-start(), calls=%async_computation.8 | async-start | bytes 2949120 | tf_op jit(solution)/shard_map/reduce_scatter | solution.py:493
  300.8 179.2 %all-reduce.5.cloned.1.call-start = ((), (), s32[]{:S(2)}) async-start(), calls=%async_computation.7 | async-start | bytes 1277952 | tf_op jit(solution)/shard_map/psum | solution.py:485
  369.3 161.4 %copy-start.3 = (f32[1,384,384]{2,1,0:T(8,128)}, f32[1,384,384]{2,1,0:T(8,128)S(1)}, u32[]{:S(2)}) copy-start(f32[1,384,384]{2,1,0:T(8,128)S(1)} %get-tuple-element.138) | copy-start | bytes 1769476
  369.3 161.4 %copy-start.4 = (f32[1,384,384]{2,1,0:T(8,128)}, f32[1,384,384]{2,1,0:T(8,128)S(1)}, u32[]{:S(2)}) copy-start(f32[1,384,384]{2,1,0:T(8,128)S(1)} %get-tuple-element.139) | copy-start | bytes 1769476
  369.3 114.2 %copy-start.2 = (f32[96,1152]{1,0:T(8,128)S(1)}, f32[96,1152]{1,0:T(8,128)}, u32[]{:S(2)}) copy-start(f32[96,1152]{1,0:T(8,128)} %param.26) | copy-start | bytes 1327108
  405.9 123.5 %copy-start.5 = (f32[1,384,384]{2,1,0:T(8,128)}, f32[1,384,384]{2,1,0:T(8,128)S(1)}, u32[]{:S(2)}) copy-start(f32[1,384,384]{2,1,0:T(8,128)S(1)} %get-tuple-element.136) | copy-start | bytes 1769476
  405.9 80.8 %copy-start.7 = (f32[96,384]{1,0:T(8,128)S(1)}, f32[96,384]{1,0:T(8,128)}, u32[]{:S(2)}) copy-start(f32[96,384]{1,0:T(8,128)} %param.29) | copy-start | bytes 442372
  483.3 5.7 %copy-start.10 = (f32[96,8]{1,0:T(8,128)S(1)}, f32[96,8]{1,0:T(8,128)}, u32[]{:S(2)}) copy-start(f32[96,8]{1,0:T(8,128)} %copy.91) | copy-start | bytes 9220
  483.3 5.7 %copy-start.11 = (f32[96,8]{1,0:T(8,128)S(1)}, f32[96,8]{1,0:T(8,128)}, u32[]{:S(2)}) copy-start(f32[96,8]{1,0:T(8,128)} %copy.89) | copy-start | bytes 9220
  483.4 5.7 %copy-start.12 = (f32[96,8]{1,0:T(8,128)S(1)}, f32[96,8]{1,0:T(8,128)}, u32[]{:S(2)}) copy-start(f32[96,8]{1,0:T(8,128)} %copy.90) | copy-start | bytes 9220
  483.5 12.2 %copy-start.17 = (f32[1,4]{0,1:T(4,128)S(1)}, f32[1,4]{0,1:T(4,128)}, u32[]{:S(2)}) copy-start(f32[1,4]{0,1:T(4,128)} %copy.101) | copy-start | bytes 52
  502.6 28.0 %copy-start.22 = (f32[7,2]{0,1:T(2,128)}, f32[7,2]{0,1:T(2,128)S(1)}, u32[]{:S(2)}) copy-start(f32[7,2]{0,1:T(2,128)S(1)} %sqrt.28) | copy-start | bytes 172
  522.8 6.6 %copy-start.6 = (f32[1,384,384]{2,1,0:T(8,128)S(1)}, f32[1,384,384]{2,1,0:T(8,128)}, u32[]{:S(2)}) copy-start(f32[1,384,384]{2,1,0:T(8,128)} %get-tuple-element.137) | copy-start | bytes 1769476
  (8 other events, 25.9 us)
Sparse Core Ops, SparseCore 0:
  13.2 20.6 all-gather.5
  71.0 17.9 all-gather.7
  91.1 17.4 all-gather.9
  299.7 31.6 reduce-scatter.3
  334.0 33.0 reduce-scatter.7
  369.5 33.0 reduce-scatter.5
  406.4 73.5 all-reduce.4

commit v2 on v1

v2 whole, which is shorter than its diff:
```python
import types

import jax
import jax.numpy as jnp
from jax import lax
from jax.experimental import pallas as pl
from jax.experimental.pallas import tpu as pltpu
from jax.sharding import PartitionSpec as P

HEADS = 6
SEQ = 197
STEP = 5
ROWS = 208
KEYS = 256
LANES = 128

beta_one = 0.9
beta_two = 0.999
adam_eps = 1e-06
decay_rate = 0.01
learn_rate = 0.4
norm_eps = 1e-06

F32 = jnp.float32
BF16 = jnp.bfloat16
VMEM = pl.BlockSpec(memory_space=pltpu.VMEM)
SMEM = pl.BlockSpec(memory_space=pltpu.SMEM)
MESH = pl.DeviceIdType.MESH


def nn(left, right):
    return lax.dot_general(left, right, (((1,), (0,)), ((), ())), preferred_element_type=F32)


def nt(left, right):
    return lax.dot_general(left, right, (((1,), (1,)), ((), ())), preferred_element_type=F32)


def tn(left, right):
    return lax.dot_general(left, right, (((0,), (0,)), ((), ())), preferred_element_type=F32)


def params(mib=58, **more):
    return pltpu.CompilerParams(vmem_limit_bytes=mib * 2**20, **more)


def ceil_to(value, step):
    return -(-value // step) * step


def normed(values):
    center = values - jnp.mean(values, axis=1, keepdims=True)
    scale = lax.rsqrt(jnp.mean(center * center, axis=1, keepdims=True) + norm_eps)
    return center * scale, scale


def lane_index(rows, lanes):
    return lax.broadcasted_iota(jnp.int32, (rows, lanes), 1)


def row_index(rows, lanes):
    return lax.broadcasted_iota(jnp.int32, (rows, lanes), 0)


def bits():
    e, h = lax.axis_index("expert"), lax.axis_index("head")
    return (e // 4, (e // 2) % 2, e % 2, h // 2, h % 2)


def device(zh, zl, y, x, c):
    return (zh * 4 + zl * 2 + y, x * 2 + c)


def flip(bit, change):
    return bit + change - 2 * bit * change


def turn(me, zh=0, zl=0, y=0, x=0, c=0):
    return tuple(flip(b, k) for b, k in zip(me, (zh, zl, y, x, c), strict=True))


def peer(me, i):
    low = (i + i // 4) % 4
    return turn(me, zl=low // 2, y=low % 2, c=i // 4)


def held_expert(where):
    return where[4] * 4 + where[1] * 2 + where[2]


def remote(src, dst, send, recv, target):
    return pltpu.make_async_remote_copy(
        src_ref=src, dst_ref=dst, send_sem=send, recv_sem=recv, device_id=target, device_id_type=MESH
    )


def greet(targets):
    barrier = pltpu.get_barrier_semaphore()
    for target in targets:
        pl.semaphore_signal(barrier, inc=1, device_id=target, device_id_type=MESH)
    pl.semaphore_wait(barrier, len(targets))


def label_matrix(experts, labels):
    row, column = row_index(LANES, LANES), lane_index(LANES, LANES)
    if labels is None:
        hit = jnp.logical_and(row == column, column < experts)
    else:
        stands = jnp.full((1, LANES), -1, jnp.int32)
        lane = lane_index(1, LANES)
        for i, e in enumerate(labels):
            stands = jnp.where(lane == i, e, stands)
        hit = row == stands
    return jnp.where(hit, 1.0, 0.0).astype(BF16)


def to_row(column, lanes):
    size = column.shape[0]
    return jnp.sum(
        jnp.where(row_index(size, lanes) == lane_index(size, lanes), column, 0.0), axis=0, keepdims=True
    )


def to_column(row, size):
    lanes = row.shape[1]
    return jnp.sum(
        jnp.where(row_index(size, lanes) == lane_index(size, lanes), row, 0.0), axis=1, keepdims=True
    )


def spread_images(images, source, wide, out):
    count = images * SEQ
    wide[0:count, :] = source[...].astype(F32)
    out[...] = jnp.zeros_like(out)
    for i in range(images):
        out[i * ROWS : i * ROWS + SEQ, :] = wide[i * SEQ : (i + 1) * SEQ, :].astype(out.dtype)


def gather_images(images, source, wide, out):
    count = images * SEQ
    for i in range(images):
        wide[i * SEQ : (i + 1) * SEQ, :] = source[i * ROWS : i * ROWS + SEQ, :]
    out[...] = wide[0:count, :].astype(out.dtype)


def route(images, experts, labels, r):
    count = images * SEQ
    total = images * ROWS
    ids = r.routes[...]
    if labels is not None:
        named_so = jnp.zeros_like(ids)
        for i, e in enumerate(labels):
            named_so = jnp.where(ids == e, i, named_so)
        ids = named_so
    r.turned[...] = jnp.zeros_like(r.turned)
    r.turned[0:2, 0:count] = ids.astype(F32)
    columns = jnp.transpose(r.turned[...])
    r.columns[...] = columns
    r.picked[...] = jnp.full(r.picked.shape, -1.0, F32)
    for i in range(images):
        r.picked[i * ROWS : i * ROWS + SEQ, :] = r.columns[i * SEQ : (i + 1) * SEQ, :]
    lane = lane_index(1, LANES)
    limits = jnp.zeros((1, LANES), F32)
    for i in range(experts):
        allowed = r.capacity[i if labels is None else labels[i]]
        limits = jnp.where(lane == i, allowed.astype(F32), limits)
    lanes = lane_index(total, LANES).astype(F32)
    one = jnp.where(lanes == r.picked[:, 0:1], 1.0, 0.0)
    two = jnp.where(lanes == r.picked[:, 1:2], 1.0, 0.0)
    firsts = jnp.sum(one, axis=0, keepdims=True)
    r.both[...] = jnp.concatenate([one.astype(BF16), two.astype(BF16)], axis=1)

    def place(i, carry):
        start = pl.multiple_of(i * ROWS, 16)
        rows = pl.ds(start, ROWS)
        lane = lane_index(ROWS, LANES).astype(F32)
        choose = r.picked[rows, :]
        hot_one = lane == choose[:, 0:1]
        hot_two = lane == choose[:, 1:2]
        before = lane_index(ROWS, total) < row_index(ROWS, total) + start
        earlier = nn(jnp.where(before, 1.0, 0.0).astype(BF16), r.both[...])
        slot = jnp.where(hot_one, earlier[:, :LANES], earlier[:, LANES:] + firsts)
        kept = jnp.logical_and(jnp.logical_or(hot_one, hot_two), slot < limits)
        r.pos[rows, :] = jnp.where(kept, slot, -1.0)
        return carry

    lax.fori_loop(0, images, place, 0)
    r.pos_rows[...] = jnp.transpose(r.pos[...])[0 : r.pos_rows.shape[0], :]


def hits(slots, total, pos_row):
    return row_index(slots, total).astype(F32) == pos_row


def project(images, r):
    total = images * ROWS
    width = r.tokens.shape[1]
    r.triple[total:, :] = jnp.zeros((r.triple.shape[0] - total, r.triple.shape[1]), BF16)
    gain, shift = r.norms[0:1, :], r.norms[1:2, :]

    def one(i, carry):
        rows = pl.ds(pl.multiple_of(i * ROWS, 16), ROWS)
        ready = (normed(r.whole[rows, :])[0] * gain + shift).astype(BF16)
        r.first[rows, :] = ready
        r.triple[rows, :] = nn(ready, r.dense[:, r.qkv_at]).astype(BF16)
        return carry

    lax.fori_loop(0, images, one, 0)


def attend_image(i, r):
    width = r.tokens.shape[1]
    head_size = width // HEADS
    scale = head_size ** (-0.5)
    low = lane_index(1, LANES) < head_size
    real = lane_index(1, KEYS) < SEQ
    spot = lane_index(1, LANES)
    zero = jnp.zeros((), BF16)
    start = pl.multiple_of(i * ROWS, 16)
    rows = pl.ds(start, ROWS)
    keys = pl.ds(start, KEYS)
    sums = jnp.zeros((ROWS, LANES), F32)
    for pair in range(HEADS // 2):
        query_at, key_at, value_at = r.spans[pair]
        query = r.triple[rows, query_at]
        key = r.triple[keys, key_at]
        value = r.triple[keys, value_at]
        blend = jnp.zeros((ROWS, LANES), F32)
        for side in range(2):
            mine = low if side == 0 else jnp.logical_not(low)
            scores = nt(query, jnp.where(mine, key, zero)) * scale
            scores = jnp.where(real, scores, -1e30)
            top = jnp.max(scores, axis=1, keepdims=True)
            expo = jnp.exp(scores - top)
            summed = jnp.sum(expo, axis=1, keepdims=True)
            sums = jnp.where(spot == pair * 2 + side, top + jnp.log(summed), sums)
            weights = (expo * (1.0 / summed)).astype(BF16)
            blend = blend + nn(weights, jnp.where(mine, value, zero))
        r.mixed[rows, pair * LANES : (pair + 1) * LANES] = blend.astype(BF16)
    r.logsum[rows, :] = sums
    after = r.whole[rows, :] + nn(r.mixed[rows, :], r.dense[:, r.proj_at])
    r.resid[rows, :] = after
    ready = (normed(after)[0] * r.norms[2:3, :] + r.norms[3:4, :]).astype(BF16)
    r.second[rows, :] = ready
    logits = nn(ready, r.router[...])
    lane = lane_index(ROWS, LANES).astype(F32)
    choose = r.picked[rows, :]
    hot_one = lane == choose[:, 0:1]
    hot_two = lane == choose[:, 1:2]
    level_one = jnp.sum(jnp.where(hot_one, logits, 0.0), axis=1, keepdims=True)
    level_two = jnp.sum(jnp.where(hot_two, logits, 0.0), axis=1, keepdims=True)
    top = jnp.maximum(level_one, level_two)
    expo_one = jnp.exp(level_one - top)
    expo_two = jnp.exp(level_two - top)
    summed = expo_one + expo_two
    r.gates[rows, :] = jnp.where(
        hot_one, expo_one / summed, jnp.where(hot_two, expo_two / summed, 0.0)
    )


def read_tail(experts, labels, r):
    width = r.dense.shape[0]
    tail = r.dense[:, 4 * width :]
    r.norms[0:4, :] = jnp.transpose(tail.astype(F32))[experts : experts + 4, :]
    r.router[...] = nn(tail, label_matrix(experts, labels)).astype(BF16)


def gelu_pair(pre):
    half = 0.5 + 0.5 * lax.erf(pre * 0.7071067811865476)
    slope = half + pre * (jnp.exp(pre * pre * -0.5) * 0.3989422804014327)
    return pre * half, slope


def expert_block(x, da, weights, tiles, keep):
    rows, width = x.shape
    answer = jnp.zeros((rows, width), F32)
    drow = jnp.zeros((rows, width), F32)
    for j in range(tiles):
        up, down = weights(j)
        hidden, slope = gelu_pair(nn(x, up))
        hidden = hidden.astype(BF16)
        dpre = (nn(da, down) * slope).astype(BF16)
        keep(j, hidden, dpre)
        answer = answer + nt(hidden, down)
        drow = drow + nt(dpre, up)
    return answer, drow


def norm_back(grad, values, gain):
    xhat, scale = normed(values)
    dgain = jnp.sum(grad * xhat, axis=0, keepdims=True)
    dshift = jnp.sum(grad, axis=0, keepdims=True)
    inner = grad * gain
    mean_one = jnp.mean(inner, axis=1, keepdims=True)
    mean_two = jnp.mean(inner * xhat, axis=1, keepdims=True)
    return (inner - mean_one - xhat * mean_two) * scale, dgain, dshift


def router_back(i, gate, dws, drow_sum, mixing, r):
    width = r.tokens.shape[1]
    rows = pl.ds(pl.multiple_of(i * ROWS, 16), ROWS)
    dchosen = gate * (dws - jnp.sum(gate * dws, axis=1, keepdims=True))
    dlogits = nt(dchosen.astype(BF16), mixing).astype(BF16)
    r.dlogits[rows, :] = dlogits
    r.dsecond[rows, :] = drow_sum + nt(dlogits, r.dense[:, 4 * width :])


def second_norm_back(i, r):
    width = r.tokens.shape[1]
    rows = pl.ds(pl.multiple_of(i * ROWS, 16), ROWS)
    dx, dgain, dshift = norm_back(r.dsecond[rows, :], r.resid[rows, :], r.norms[2:3, :])
    dx = dx + r.dpad[rows, :].astype(F32)
    r.small[2:3, :] += dgain
    r.small[3:4, :] += dshift
    r.dres[rows, :] = dx
    dattn = dx.astype(BF16)
    r.dattn[rows, :] = dattn
    r.dmix[rows, :] = nt(dattn, r.dense[:, r.proj_at]).astype(BF16)


def attend_back(i, pair, r):
    width = r.tokens.shape[1]
    head_size = width // HEADS
    scale = head_size ** (-0.5)
    low = lane_index(1, LANES) < head_size
    real = lane_index(1, KEYS) < SEQ
    zero = jnp.zeros((), BF16)
    start = pl.multiple_of(i * ROWS, 16)
    rows = pl.ds(start, ROWS)
    keys = pl.ds(start, KEYS)
    query_at, key_at, value_at = r.spans[pair]
    sums = r.logsum[rows, :]
    query = r.triple[rows, query_at]
    key = r.triple[keys, key_at]
    value = r.triple[keys, value_at]
    dm = r.dmix[rows, pair * LANES : (pair + 1) * LANES]
    dq = jnp.zeros((ROWS, LANES), F32)
    dk = jnp.zeros((KEYS, LANES), F32)
    dv = jnp.zeros((KEYS, LANES), F32)
    for side in range(2):
        mine = low if side == 0 else jnp.logical_not(low)
        head = pair * 2 + side
        key_mine = jnp.where(mine, key, zero)
        dm_mine = jnp.where(mine, dm, zero)
        scores = nt(query, key_mine) * scale
        probs = jnp.where(real, jnp.exp(scores - sums[:, head : head + 1]), 0.0)
        dprobs = nt(dm_mine, value)
        inner = jnp.sum(dprobs * probs, axis=1, keepdims=True)
        dscores = (probs * (dprobs - inner)).astype(BF16)
        dv = dv + tn(probs.astype(BF16), dm_mine)
        dq = dq + nn(dscores, key_mine)
        dk = dk + tn(dscores, jnp.where(mine, query, zero))
    r.dtriple[rows, query_at] = (dq * scale).astype(BF16)
    r.dtriple[rows, key_at] = (dk * scale)[:ROWS].astype(BF16)
    r.dtriple[rows, value_at] = dv[:ROWS].astype(BF16)


def first_norm_back(i, r):
    width = r.tokens.shape[1]
    rows = pl.ds(pl.multiple_of(i * ROWS, 16), ROWS)
    dfirst = nt(r.dtriple[rows, :], r.dense[:, r.qkv_at])
    dx, dgain, dshift = norm_back(dfirst, r.whole[rows, :], r.norms[0:1, :])
    r.small[0:1, :] += dgain
    r.small[1:2, :] += dshift
    r.dres[rows, :] += dx


def tail_grads(experts, r):
    width = r.tokens.shape[1]
    tail = tn(r.second[...], r.dlogits[...])
    columns = jnp.transpose(
        jnp.concatenate([r.small[...], jnp.zeros((LANES - 8, width), F32)], axis=0)
    )
    shifted = pltpu.roll(columns, experts, 1)
    return jnp.where(lane_index(width, LANES) < experts, tail, shifted)


def natural_layout(width):
    return types.SimpleNamespace(
        spans=natural_spans(width), qkv_at=slice(0, 3 * width), proj_at=slice(3 * width, 4 * width)
    )


def natural_spans(width):
    return [
        tuple(slice(k * width + pair * LANES, k * width + (pair + 1) * LANES) for k in range(3))
        for pair in range(HEADS // 2)
    ]


def paired_spans():
    return [
        tuple(slice((pair * 3 + k) * LANES, (pair * 3 + k + 1) * LANES) for k in range(3))
        for pair in range(HEADS // 2)
    ]


def adam_terms(weight, grad, first, second):
    new_first = beta_one * first + (1.0 - beta_one) * grad
    new_second = beta_two * second + (1.0 - beta_two) * grad * grad
    corr_one = 1.0 - beta_one**STEP
    corr_two = 1.0 - beta_two**STEP
    update = (
        new_first / corr_one / (jnp.sqrt(new_second / corr_two) + adam_eps) + decay_rate * weight
    )
    return (new_first, new_second, update)


def take_saved(r, refs):
    (r.first, r.triple, r.logsum, r.mixed, r.resid, r.second, r.pos, r.gates) = refs


def saved_shapes(total, width):
    return (
        ((total, width), BF16),
        ((total + KEYS - ROWS, 3 * width), BF16),
        ((total, LANES), F32),
        ((total, width), BF16),
        ((total, width), F32),
        ((total, width), BF16),
        ((total, LANES), F32),
        ((total, LANES), F32),
    )


def take_route(r, refs):
    (
        r.turned, r.columns, r.picked, r.both, r.pos_rows, r.whole, r.dpad, r.wide, r.norms, r.router,
    ) = refs


def route_shapes(count, total, width, experts):
    padded = ceil_to(count, LANES)
    return (
        ((LANES, padded), F32),
        ((padded, LANES), F32),
        ((total, LANES), F32),
        ((total, 2 * LANES), BF16),
        ((ceil_to(experts, 8), total), F32),
        ((total, width), F32),
        ((total, width), BF16),
        ((ceil_to(count, 8), width), F32),
        ((8, width), F32),
        ((width, LANES), BF16),
    )


def structs(shapes):
    return tuple(jax.ShapeDtypeStruct(*one) for one in shapes)


def buffers(shapes):
    return [pltpu.VMEM(*one) for one in shapes]


def plain_attend(tokens, dout, routes, capacity, dense, slots):
    count, width = tokens.shape
    experts = capacity.shape[0]
    images = count // SEQ
    total = images * ROWS
    shape = jax.ShapeDtypeStruct

    def body(*refs):
        r = natural_layout(width)
        (r.tokens, r.dout, r.routes, r.capacity, r.dense) = refs[:5]
        take_saved(r, refs[5:13])
        r.sent, r.weight_rows = refs[13], refs[-1]
        take_route(r, refs[14:-1])
        spread_images(images, r.tokens, r.wide, r.whole)
        spread_images(images, r.dout, r.wide, r.dpad)
        read_tail(experts, None, r)
        route(images, experts, None, r)
        project(images, r)

        def image(i, carry):
            attend_image(i, r)
            return carry

        lax.fori_loop(0, images, image, 0)
        weighted = jnp.where(r.pos[...] >= 0.0, r.gates[...], 0.0)
        r.weight_rows[...] = jnp.transpose(weighted)[0 : r.weight_rows.shape[0], :]

        def dispatch(e, carry):
            hit = hits(slots, total, r.pos_rows[pl.ds(e, 1), :])
            share = jnp.sum(jnp.where(hit, r.weight_rows[pl.ds(e, 1), :], 0.0), axis=1, keepdims=True)
            place = jnp.where(hit, 1.0, 0.0).astype(BF16)
            r.sent[e, :, 0:width] = nn(place, r.second[...]).astype(BF16)
            r.sent[e, :, width:] = (nn(place, r.dpad[...]) * share).astype(BF16)
            return carry

        lax.fori_loop(0, experts, dispatch, 0)

    return pl.pallas_call(
        body,
        out_shape=structs(saved_shapes(total, width)) + (shape((experts, slots, 2 * width), BF16),),
        in_specs=[VMEM, VMEM, VMEM, SMEM, VMEM],
        out_specs=(VMEM,) * 9,
        scratch_shapes=buffers(route_shapes(count, total, width, experts))
        + [pltpu.VMEM((ceil_to(experts, 8), total), F32)],
        compiler_params=params(),
        name="attend",
    )(tokens, dout, routes, capacity, dense)


def plain_expert(arrived, up, down):
    rows = arrived.shape[0]
    width, hidden_size = up.shape
    chunk = 320
    while rows % chunk:
        chunk -= 16
    tile = 512
    shape = jax.ShapeDtypeStruct

    def body(*refs):
        r = types.SimpleNamespace()
        (r.arrived, r.up, r.down, r.back, r.grad_up, r.grad_down, r.hiddens, r.dpres) = refs

        def block(b, carry):
            at = pl.ds(pl.multiple_of(b * chunk, 16), chunk)

            def weights(j):
                cols = slice(j * tile, (j + 1) * tile)
                return r.up[:, cols], r.down[:, cols]

            def keep(j, hidden, dpre):
                r.hiddens[at, j * tile : (j + 1) * tile] = hidden
                r.dpres[at, j * tile : (j + 1) * tile] = dpre

            answer, drow = expert_block(
                r.arrived[at, 0:width], r.arrived[at, width:], weights, hidden_size // tile, keep
            )
            r.back[at, 0:width] = answer.astype(BF16)
            r.back[at, width:] = drow.astype(BF16)
            return carry

        lax.fori_loop(0, rows // chunk, block, 0)

        def grads(j, carry):
            cols = pl.ds(pl.multiple_of(j * 256, 256), 256)
            r.grad_up[:, cols] = tn(r.arrived[:, 0:width], r.dpres[:, cols])
            r.grad_down[:, cols] = tn(r.arrived[:, width:], r.hiddens[:, cols])
            return carry

        lax.fori_loop(0, hidden_size // 256, grads, 0)

    return pl.pallas_call(
        body,
        out_shape=(
            shape((rows, 2 * width), BF16),
            shape((width, hidden_size), F32),
            shape((width, hidden_size), F32),
        ),
        in_specs=[VMEM] * 3,
        out_specs=(VMEM,) * 3,
        scratch_shapes=[pltpu.VMEM((rows, hidden_size), BF16)] * 2,
        compiler_params=params(),
        name="expert",
    )(arrived, up, down)


def plain_backward(tokens, dout, dense, saved, back):
    count, width = tokens.shape
    experts, slots, _ = back.shape
    images = count // SEQ
    total = images * ROWS
    shape = jax.ShapeDtypeStruct

    def body(*refs):
        r = natural_layout(width)
        (r.tokens, r.dout, r.dense) = refs[:3]
        take_saved(r, refs[3:11])
        (r.back, r.output, r.input_grad, r.grads) = refs[11:15]
        (
            r.wide, r.whole, r.dpad, r.dlogits, r.dsecond, r.dtriple,
            r.dres, r.dattn, r.dmix, r.small, r.norms, r.router, r.outs,
        ) = refs[15:]
        spread_images(images, r.tokens, r.wide, r.whole)
        spread_images(images, r.dout, r.wide, r.dpad)
        read_tail(experts, None, r)
        mixing = label_matrix(experts, None)
        lane = lane_index(ROWS, LANES)
        slot = lane_index(ROWS, slots).astype(F32)

        def combine(i, carry):
            rows = pl.ds(pl.multiple_of(i * ROWS, 16), ROWS)
            dhere = r.dpad[rows, :].astype(F32)
            gate = r.gates[rows, :]
            spots = r.pos[rows, :]

            def one(e, sums):
                out, dws, dr = sums
                mine = lane == e
                at = jnp.sum(jnp.where(mine, spots, 0.0), axis=1, keepdims=True)
                share = jnp.sum(jnp.where(mine, gate, 0.0), axis=1, keepdims=True)
                place = jnp.where(slot == at, 1.0, 0.0).astype(BF16)
                both = nn(place, r.back[e])
                answer = both[:, 0:width]
                out = out + share * answer
                dws = jnp.where(mine, jnp.sum(dhere * answer, axis=1, keepdims=True), dws)
                return (out, dws, dr + both[:, width:])

            start = (r.resid[rows, :], jnp.zeros((ROWS, LANES), F32), jnp.zeros((ROWS, width), F32))
            out, dws, dr = lax.fori_loop(0, experts, one, start)
            r.outs[rows, :] = out
            router_back(i, gate, dws, dr, mixing, r)
            return carry

        lax.fori_loop(0, images, combine, 0)
        gather_images(images, r.outs, r.wide, r.output)
        r.small[...] = jnp.zeros_like(r.small)

        def middle(i, carry):
            second_norm_back(i, r)
            return carry

        lax.fori_loop(0, images, middle, 0)

        def image(i, carry):
            for pair in range(HEADS // 2):
                attend_back(i, pair, r)
            first_norm_back(i, r)
            return carry

        lax.fori_loop(0, images, image, 0)
        gather_images(images, r.dres, r.wide, r.input_grad)
        r.grads[:, 3 * width : 4 * width] = tn(r.mixed[...], r.dattn[...])
        r.grads[:, 4 * width :] = tail_grads(experts, r)
        for k in range(3):
            cols = slice(k * width, (k + 1) * width)
            r.grads[:, cols] = tn(r.first[...], r.dtriple[:, cols])

    return pl.pallas_call(
        body,
        out_shape=(
            shape((count, width), BF16),
            shape((count, width), BF16),
            shape((width, 4 * width + LANES), F32),
        ),
        in_specs=[VMEM] * 12,
        out_specs=(VMEM,) * 3,
        scratch_shapes=buffers(
            (
                ((ceil_to(count, 8), width), F32),
                ((total, width), F32),
                ((total, width), BF16),
                ((total, LANES), BF16),
                ((total, width), F32),
                ((total, 3 * width), BF16),
                ((total, width), F32),
                ((total, width), BF16),
                ((total, width), BF16),
                ((8, width), F32),
                ((8, width), F32),
                ((width, LANES), BF16),
                ((total, width), F32),
            )
        ),
        compiler_params=params(),
        name="backward",
    )(tokens, dout, dense, *saved, back)


def squares(values):
    return jnp.sum(values * values)


def plain_step(
    block_input, out_cotangent, route_ids, capacity,
    qkv_weight, qkv_first, qkv_second,
    proj_weight, proj_first, proj_second,
    router_weight, router_first, router_second,
    norm_params, norm_first, norm_second,
    expert_up, up_first, up_second,
    expert_down, down_first, down_second,
):
    count, width = block_input.shape
    experts = router_weight.shape[1]
    slots = ceil_to(max(2, 3 * count // lax.axis_size("expert")), 16)
    rows_dev = qkv_weight.shape[0]
    dense = jnp.concatenate(
        [qkv_weight, proj_weight, router_weight, norm_params,
         jnp.zeros((rows_dev, LANES - experts - 4), F32)], axis=1
    ).astype(BF16)
    dense = lax.all_gather(dense, "head", axis=0, tiled=True)
    up_w = lax.all_gather(expert_up[0].astype(BF16), "head", axis=1, tiled=True)
    down_w = lax.all_gather(expert_down[0].astype(BF16), "head", axis=1, tiled=True)
    *saved, sent = plain_attend(block_input, out_cotangent, route_ids.T, capacity, dense, slots)
    arrived = lax.all_to_all(sent, "expert", split_axis=0, concat_axis=0, tiled=True)
    back, grad_up, grad_down = plain_expert(arrived.reshape(experts * slots, 2 * width), up_w, down_w)
    back = lax.all_to_all(
        back.reshape(experts, slots, 2 * width), "expert", split_axis=0, concat_axis=0, tiled=True
    )
    block_output, input_grad, grads = plain_backward(block_input, out_cotangent, dense, saved, back)
    summed = lax.psum_scatter(grads, "head", scatter_dimension=0, tiled=True)
    summed = lax.psum(summed, "expert")
    shares = (
        summed[:, 0 : 3 * width],
        summed[:, 3 * width : 4 * width],
        summed[:, 4 * width : 4 * width + experts],
        summed[:, 4 * width + experts : 4 * width + experts + 4],
    )
    expert_grads = (
        lax.psum_scatter(grad_up, "head", scatter_dimension=1, tiled=True),
        lax.psum_scatter(grad_down, "head", scatter_dimension=1, tiled=True),
    )
    qkv_m, qkv_v, qkv_r = adam_terms(qkv_weight, shares[0], qkv_first, qkv_second)
    proj_m, proj_v, proj_r = adam_terms(proj_weight, shares[1], proj_first, proj_second)
    router_m, router_v, router_r = adam_terms(router_weight, shares[2], router_first, router_second)
    norm_m, norm_v, norm_r = adam_terms(norm_params, shares[3], norm_first, norm_second)
    up_m, up_v, up_r = adam_terms(expert_up, expert_grads[0][None], up_first, up_second)
    down_m, down_v, down_r = adam_terms(expert_down, expert_grads[1][None], down_first, down_second)
    weight_col = jnp.concatenate(
        [
            jnp.stack([squares(qkv_weight), squares(proj_weight), squares(router_weight)]),
            jnp.sum(norm_params * norm_params, axis=0),
        ]
    )
    update_col = jnp.concatenate(
        [
            jnp.stack([squares(qkv_r), squares(proj_r), squares(router_r)]),
            jnp.sum(norm_r * norm_r, axis=0),
        ]
    )
    expert_sq = jnp.stack(
        [squares(expert_up), squares(up_r), squares(expert_down), squares(down_r)]
    )[None, :]
    totals = lax.psum((jnp.stack([weight_col, update_col], axis=1), expert_sq), "head")
    dense_norms = jnp.sqrt(totals[0])
    expert_norms = jnp.sqrt(totals[1])
    trust = dense_norms[:, 0] / dense_norms[:, 1]
    qkv_new = qkv_weight - learn_rate * trust[0] * qkv_r
    proj_new = proj_weight - learn_rate * trust[1] * proj_r
    router_new = router_weight - learn_rate * trust[2] * router_r
    norm_new = norm_params - learn_rate * trust[3:][None, :] * norm_r
    up_new = expert_up - learn_rate * (expert_norms[0, 0] / expert_norms[0, 1]) * up_r
    down_new = expert_down - learn_rate * (expert_norms[0, 2] / expert_norms[0, 3]) * down_r
    return (
        block_output, input_grad,
        qkv_new, qkv_new.astype(BF16), qkv_m, qkv_v,
        proj_new, proj_new.astype(BF16), proj_m, proj_v,
        router_new, router_new.astype(BF16), router_m, router_v,
        norm_new, norm_new.astype(BF16), norm_m, norm_v,
        up_new, up_new.astype(BF16), up_m, up_v,
        down_new, down_new.astype(BF16), down_m, down_v,
        dense_norms, expert_norms,
    )


UNITS = 8
GROUP = 4


def arrival(ref, sem, target):
    remote(ref, ref, sem, sem, target).wait_recv()


def block(ref, i, size):
    return ref.at[pl.ds(pl.multiple_of(i * size, 8), size), :]


def total_of(values):
    return jnp.sum(jnp.sum(values * values, axis=1, keepdims=True), axis=0, keepdims=True)


def dense_order(width):
    spans = paired_spans()
    qkv = [spans[j % 3][j // 3] for j in range(9)]
    return (
        [slice(width + at.start, width + at.stop) for at in qkv]
        + [slice(j * LANES, (j + 1) * LANES) for j in range(3)]
        + [slice(4 * width, 4 * width + LANES)]
    )


def core_inputs(r, refs):
    (
        r.tokens, r.dout, r.routes, r.capacity,
        r.qkv_w, r.proj_w, r.router_w, r.norm_w, r.up_w, r.down_w,
        r.router_m, r.router_v, r.norm_m, r.norm_v,
        r.qkv_m_hbm, r.qkv_v_hbm, r.proj_m_hbm, r.proj_v_hbm,
        r.up_m_hbm, r.up_v_hbm, r.down_m_hbm, r.down_v_hbm,
    ) = refs


def core_outputs(r, refs):
    (r.output, r.input_grad, r.sum_recv, r.full, r.norm_row) = refs


def core_scratch(r, refs):
    (
        r.dense, r.ups, r.downs, r.own_up, r.own_down, r.square,
        r.rows, r.shares, r.douts, r.das, r.dsend, r.x, r.share, r.ssend, r.drows, r.dshares, r.arrived,
        r.hiddens, r.dpres, r.kept, r.given, r.side, r.sum_send,
        r.dsecond, r.dres, r.small, r.chunk, r.mine, r.head_out, r.head_in, r.quad_out, r.quad_in, r.half_out, r.half_in,
        r.tallies, r.qkv_m, r.qkv_v, r.proj_m, r.proj_v,
    ) = refs


def core_semaphores(r, refs):
    (
        r.dense_send, r.dense_recv, r.side_send, r.far_send, r.on_send, r.up_recv, r.down_recv,
        r.t_send, r.t_recv, r.x_send, r.x_recv, r.w_send, r.w_recv, r.d_send, r.d_recv, r.s_send, r.s_recv,
        r.a_send, r.a_recv, r.g_send, r.g_recv, r.f_send, r.f_recv,
        r.head_send, r.head_recv, r.quad_send, r.quad_recv, r.half_send, r.half_recv, r.full_send, r.full_recv,
        r.n_send, r.n_recv, r.load,
    ) = refs


def paired_core(tokens, dout, routes, capacity, weights, small_moments, moments, slots):
    count, width = tokens.shape
    images = count // SEQ
    total = images * ROWS
    rows_dev = weights[0].shape[0]
    piece = weights[4].shape[1]
    wide_dense = 4 * width + LANES
    chunks = [(j * width, width) for j in range(4)] + [(4 * width, 2 * LANES)]
    shots = [(0, 2 * width), (2 * width, 2 * width), (4 * width, 2 * LANES)]
    shot_chunks = [(0, 1), (2, 3), (4,)]
    wide_grads = 4 * width + 2 * LANES
    part = rows_dev // 2
    saved = saved_shapes(total, width)
    routing = route_shapes(count, total, width, UNITS)

    def body(*refs):
        r = types.SimpleNamespace(
            spans=paired_spans(), proj_at=slice(0, width), qkv_at=slice(width, 4 * width)
        )
        refs = list(refs)

        def take(n):
            taken = refs[:n]
            del refs[:n]
            return taken

        core_inputs(r, take(22))
        core_outputs(r, take(5))
        take_saved(r, take(len(saved)))
        take_route(r, take(len(routing)))
        core_scratch(r, take(39))
        core_semaphores(r, refs)
        r.dtriple = r.hiddens.at[0:total, 0 : 3 * width]
        r.dattn = r.hiddens.at[0:total, 3 * width : 4 * width]
        r.dmix = r.dpres.at[0:total, 0:width]
        r.dlogits = r.dpres.at[0:total, width : width + LANES]
        r.dws = r.picked

        me = bits()
        zh, zl, y, x, c = me
        h = x * 2 + c
        sibling, across = device(*turn(me, c=1)), device(*turn(me, x=1))
        corner = device(*turn(me, x=1, c=1))
        far = device(1 - zh, zl, y, x, zh)
        far_cores = [device(1 - zh, zl, y, x, k) for k in range(2)]
        labels = [held_expert(peer(me, i)) for i in range(UNITS)]
        targets = [device(*peer(me, i)) for i in range(UNITS)]
        quad = [turn(me, zl=m // 2, y=m % 2) for m in range(4)]
        quad_targets = [device(*there) for there in quad]
        opposite = device(*turn(me, zh=1))

        barrier = pltpu.get_barrier_semaphore()
        greeted = targets[1:] + [across, corner, opposite, device(*turn(me, zh=1, c=1))]
        for target in greeted:
            pl.semaphore_signal(barrier, inc=1, device_id=target, device_id_type=MESH)

        loads = [
            pltpu.make_async_copy(src, dst, r.load.at[k])
            for k, (src, dst) in enumerate(
                ((r.qkv_m_hbm, r.qkv_m), (r.qkv_v_hbm, r.qkv_v), (r.proj_m_hbm, r.proj_m), (r.proj_v_hbm, r.proj_v))
            )
        ]
        for copy in loads:
            copy.start()

        mine = pl.ds(pl.multiple_of(h * rows_dev, 16), rows_dev)
        order = dense_order(width)
        for j in range(9):
            r.dense[mine, order[j]] = r.qkv_w[:, j * LANES : (j + 1) * LANES].astype(BF16)
        r.dense[mine, r.proj_at] = r.proj_w[...].astype(BF16)
        r.square[...] = jnp.zeros_like(r.square)
        r.square[0:UNITS, 0:rows_dev] = r.router_w[...]
        r.square[UNITS : UNITS + 4, 0:rows_dev] = r.norm_w[...]
        r.dense[mine, 4 * width :] = jnp.transpose(r.square[...])[0:rows_dev, :].astype(BF16)
        r.own_up[...] = r.up_w[...].astype(BF16)
        r.own_down[...] = r.down_w[...].astype(BF16)
        parts = ((r.own_up, r.ups, r.up_recv), (r.own_down, r.downs, r.down_recv))

        @pl.when(c == zh)
        def _():
            for own, whole, _ in parts:
                whole[h] = own[...]

        pl.semaphore_wait(barrier, len(greeted))
        pending = []

        def start(copy):
            copy.start()
            pending.append(copy.wait_send)

        def when(condition, *calls):
            @pl.when(condition)
            def _():
                for call in calls:
                    call()

        def start_where(condition, copies):
            when(condition, *[copy.start for copy in copies])
            pending.append(lambda: when(condition, *[copy.wait_send for copy in copies]))

        def dense_rows(q):
            return r.dense.at[pl.ds(pl.multiple_of(q * rows_dev, 16), rows_dev), :]

        start(remote(dense_rows(h), dense_rows(h), r.dense_send.at[0], r.dense_recv.at[h], across))
        start(remote(dense_rows(h), dense_rows(h), r.dense_send.at[1], r.dense_recv.at[h], sibling))
        side = [
            remote(own, whole.at[h], r.side_send.at[p], recv.at[h], sibling)
            for p, (own, whole, recv) in enumerate(parts)
        ]

        start_where(c != zh, side)
        for p, (own, whole, recv) in enumerate(parts):
            start(remote(own, whole.at[h], r.far_send.at[p], recv.at[h], far))

        spread_images(images, r.tokens, r.wide, r.whole)
        spread_images(images, r.dout, r.wide, r.dpad)
        route(images, UNITS, labels, r)

        def placed(i):
            hit = hits(slots, total, r.pos_rows[i : i + 1, :])
            return hit, jnp.where(hit, 1.0, 0.0).astype(BF16)

        dout_sends = []
        for i in range(UNITS):
            filled = nn(placed(i)[1], r.dpad[...]).astype(BF16)
            if i == 0:
                r.douts[0:slots, :] = filled
            else:
                r.dsend[i * slots : (i + 1) * slots, :] = filled
                dout_sends.append(
                    remote(
                        block(r.dsend, i, slots), block(r.douts, i, slots),
                        r.t_send.at[i], r.t_recv.at[i], targets[i],
                    )
                )
                dout_sends[-1].start()

        next_q = (1 - x) * 2 + c
        arrival(dense_rows(next_q), r.dense_recv.at[next_q], across)
        start(
            remote(dense_rows(next_q), dense_rows(next_q), r.dense_send.at[2], r.dense_recv.at[next_q], sibling)
        )

        def onward(p):
            own, whole, recv = parts[p]
            return [
                remote(whole.at[x * 2 + k], whole.at[x * 2 + k], r.on_send.at[p * 2 + k], recv.at[x * 2 + k], across)
                for k in range(2)
            ]

        @pl.when(c == zh)
        def _():
            for p in range(2):
                other = x * 2 + 1 - c
                arrival(parts[p][1].at[other], parts[p][2].at[other], sibling)
                for copy in onward(p):
                    copy.start()

        pending.extend(copy.wait_send for p in range(2) for copy in onward(p))
        for q in (x * 2 + 1 - c, (1 - x) * 2 + 1 - c):
            arrival(dense_rows(q), r.dense_recv.at[q], sibling)
        read_tail(UNITS, labels, r)
        project(images, r)

        def far_arrived(p):
            for k in range(2):
                arrival(parts[p][1].at[x * 2 + k], parts[p][2].at[x * 2 + k], far)
            for copy in onward(p):
                copy.start()

        def image(i, carry):
            attend_image(i, r)

            @pl.when(jnp.logical_and(c != zh, i == images // 2))
            def _():
                far_arrived(0)

            return carry

        lax.fori_loop(0, images, image, 0)


        def out_copies(i, target):
            return (
                remote(block(r.rows, i, slots), block(r.x, i, slots), r.x_send.at[i], r.x_recv.at[i], target),
                remote(block(r.shares, i, 8), block(r.share, i, 8), r.w_send.at[i], r.w_recv.at[i], target),
            )

        def back_copies(i, target):
            return (
                remote(block(r.dsend, i, slots), block(r.drows, i, slots), r.d_send.at[i], r.d_recv.at[i], target),
                remote(block(r.ssend, i, 8), block(r.dshares, i, 8), r.s_send.at[i], r.s_recv.at[i], target),
            )

        weight_rows = jnp.transpose(jnp.where(r.pos[...] >= 0.0, r.gates[...], 0.0))
        for i in (*range(1, UNITS), 0):
            hit, place = placed(i)
            share = jnp.sum(jnp.where(hit, weight_rows[i : i + 1, :], 0.0), axis=1, keepdims=True)
            share = jnp.broadcast_to(to_row(share, width), (8, width))
            filled = nn(place, r.second[...]).astype(BF16)
            if i == 0:
                r.share[0:8, :] = share
                r.x[0:slots, :] = filled
            else:
                r.shares[i * 8 : (i + 1) * 8, :] = share
                r.rows[i * slots : (i + 1) * slots, :] = filled
                for copy in out_copies(i, targets[i]):
                    copy.start()

        @pl.when(c != zh)
        def _():
            far_arrived(1)

        for copy in dout_sends:
            copy.wait_send()


        def expert_rows(i):
            return (
                pl.ds(pl.multiple_of(i * slots, 16), slots),
                pl.ds(pl.multiple_of((i % GROUP) * slots, 16), slots),
                pl.ds(pl.multiple_of(i * 8, 8), 8),
                device(*peer(me, i)),
            )

        def ready(i):
            at, _, small, target = expert_rows(i)

            @pl.when(i > 0)
            def _():
                arrival(block(r.douts, i, slots), r.t_recv.at[i], target)
                for copy in out_copies(i, target):
                    copy.wait()

            d = r.douts[at, :].astype(F32)
            r.das[at, :] = (d * to_column(r.share[small, :][0:1, :], slots)).astype(BF16)

        def part_of(i, which):
            at, within, _, _ = expert_rows(i)

            def weights(k):
                return r.ups[which * 2 + k], r.downs[which * 2 + k]

            def keep(k, hidden, dpre):
                cols = pl.ds(pl.multiple_of((which * 2 + k) * piece, LANES), piece)
                r.hiddens[within, cols] = hidden
                r.dpres[within, cols] = dpre

            return expert_block(r.x[at, :], r.das[at, :], weights, 2, keep)

        def all_of(i):
            at, within, _, _ = expert_rows(i)

            def weights(q):
                return r.ups[q], r.downs[q]

            def keep(q, hidden, dpre):
                r.hiddens[within, q * piece : (q + 1) * piece] = hidden
                r.dpres[within, q * piece : (q + 1) * piece] = dpre

            return expert_block(r.x[at, :], r.das[at, :], weights, 4, keep)

        def done(i, answer, drow):
            at, _, small, target = expert_rows(i)
            answer = answer.astype(BF16)
            r.rows[at, :] = answer
            r.dsend[at, :] = drow.astype(BF16)
            dshare = jnp.sum(r.douts[at, :].astype(F32) * answer.astype(F32), axis=1, keepdims=True)
            r.ssend[small, :] = jnp.broadcast_to(to_row(dshare, width), (8, width))

            @pl.when(i > 0)
            def _():
                for copy in back_copies(i, target):
                    copy.start()

        def early(i, carry):
            ready(i)
            answer, drow = part_of(i, x)
            r.kept[i, 0:slots, 0:width] = answer
            r.kept[i, 0:slots, width:] = drow
            return carry

        def late(i, carry):
            answer, drow = part_of(i, 1 - x)
            done(i, answer + r.kept[i, 0:slots, 0:width], drow + r.kept[i, 0:slots, width:])
            return carry

        def one(i, carry):
            ready(i)
            answer, drow = all_of(i)
            done(i, answer, drow)
            return carry

        halves = [slice(p * piece, (p + 1) * piece) for p in range(2)]

        def over_x(p, k):
            return remote(
                r.given.at[k, :, halves[p]], r.side.at[k, :, halves[p]],
                r.g_send.at[p * 2 + k], r.g_recv.at[p * 2 + k], across,
            )

        def add_grads(g, x_of, k):
            at = pl.ds(g * GROUP * slots, GROUP * slots)
            cols = pl.ds(pl.multiple_of((x_of * 2 + k) * piece, LANES), piece)
            both = (tn(r.x[at, :], r.dpres[:, cols]), tn(r.das[at, :], r.hiddens[:, cols]))
            q = x_of * 2 + k
            if g == 0:
                for p in range(2):
                    r.kept[q, :, halves[p]] = both[p]
            elif x_of is x:
                for p in range(2):
                    r.kept[q, :, halves[p]] += both[p]
            else:
                for p in range(2):
                    r.given[k, :, halves[p]] = (r.kept[q, :, halves[p]] + both[p]).astype(BF16)
                    start(over_x(p, k))

        other_x = 1 - x
        for g in range(UNITS // GROUP):
            if g == 0:
                for p in range(2):
                    for k in range(2):
                        q = other_x * 2 + k
                        arrival(parts[p][1].at[q], parts[p][2].at[q], across)
            lax.fori_loop(g * GROUP, (g + 1) * GROUP, one, 0)
            for x_of in (other_x, x):
                for k in range(2):
                    add_grads(g, x_of, k)
        pending.extend(copy.wait_send for i in range(1, UNITS) for copy in back_copies(i, targets[i]))


        r.arrived[0:slots, :] = r.rows[0:slots, :]
        r.drows[0:slots, :] = r.dsend[0:slots, :]
        r.dshares[0:8, :] = r.ssend[0:8, :]
        lane = lane_index(ROWS, LANES)
        slot = lane_index(ROWS, slots).astype(F32)

        for i in range(1, UNITS):
            for copy in back_copies(i, targets[i]):
                copy.wait_recv()

        def combine(i, carry):
            rows = pl.ds(pl.multiple_of(i * ROWS, 16), ROWS)
            spots = r.pos[rows, :]
            dws = jnp.zeros((ROWS, LANES), F32)
            dr = jnp.zeros((ROWS, width), F32)
            for e in range(UNITS):
                hit = slot == spots[:, e : e + 1]
                found = jnp.where(hit, r.dshares[e * 8 : e * 8 + 1, 0:slots], 0.0)
                dws = jnp.where(lane == e, jnp.sum(found, axis=1, keepdims=True), dws)
                place = jnp.where(hit, 1.0, 0.0).astype(BF16)
                dr = dr + nn(place, r.drows[e * slots : (e + 1) * slots, :])
            r.dws[rows, :] = dws
            r.dsecond[rows, :] = dr
            return carry

        for i in range(1, UNITS):
            start(
                remote(
                    block(r.rows, i, slots), block(r.arrived, i, slots),
                    r.a_send.at[i], r.a_recv.at[i], targets[i],
                )
            )

        lax.fori_loop(0, images, combine, 0)


        def sums(p, k, target, at):
            return remote(
                r.sum_send.at[k, :, halves[p]], r.sum_recv.at[at, :, halves[p]],
                r.f_send.at[p * 2 + k], r.f_recv.at[p * 2 + at], target,
            )

        def after_x(k):
            for p in range(2):
                over_x(p, k).wait_recv()
                there = r.kept[x * 2 + k, :, halves[p]] + r.side[k, :, halves[p]].astype(F32)
                r.sum_send[k, :, halves[p]] = there.astype(BF16)
                start_where(jnp.logical_and(c == zh, c != k), [sums(p, k, sibling, 0)])
                start_where(c != zh, [sums(p, k, far_cores[k], 1)])

            @pl.when(jnp.logical_and(c == zh, c == k))
            def _():
                r.sum_recv[0] = r.sum_send[k]

        after_x(0)


        mixing = label_matrix(UNITS, labels)
        r.small[...] = jnp.zeros_like(r.small)

        def middle(i, carry):
            rows = pl.ds(pl.multiple_of(i * ROWS, 16), ROWS)
            router_back(i, r.gates[rows, :], r.dws[rows, :], r.dsecond[rows, :], mixing, r)
            second_norm_back(i, r)
            return carry

        lax.fori_loop(0, images, middle, 0)


        relations = (sibling, across, corner)
        related = (x * 2 + 1 - c, (1 - x) * 2 + c, (1 - x) * 2 + 1 - c)

        def head_copy(j, k):
            at, size = chunks[j]
            cols = slice(at, at + size)
            return remote(
                r.head_out.at[k, :, cols], r.head_in.at[k, :, cols],
                r.head_send.at[j * 3 + k], r.head_recv.at[j * 3 + k], relations[k],
            )

        def over_head(j, grads):
            at, size = chunks[j]
            cols = slice(at, at + size)
            r.chunk[:, 0:size] = grads
            for k in range(3):
                rows = pl.ds(pl.multiple_of(related[k] * rows_dev, 16), rows_dev)
                r.head_out[k, :, cols] = r.chunk[rows, 0:size].astype(BF16)
                start(head_copy(j, k))
            r.mine[:, cols] = r.chunk[mine, 0:size]

        def quarter(s, there):
            at, size = shots[s]
            rows = pl.ds(pl.multiple_of(there[2] * part, 16), part)
            return rows, pl.ds(pl.multiple_of(at + there[1] * (size // 2), LANES), size // 2)

        def first_of(s):
            at, size = shots[s]
            return slice(at // 2, (at + size) // 2)

        def quad_copy(s, m):
            return remote(
                r.quad_out.at[*quarter(s, quad[m])], r.quad_in.at[m, :, first_of(s)],
                r.quad_send.at[s * 4 + m], r.quad_recv.at[s * 4 + m], quad_targets[m],
            )

        def over_quad(s):
            for j in shot_chunks[s]:
                at, size = chunks[j]
                cols = slice(at, at + size)
                summed = r.mine[:, cols]
                for k in range(3):
                    head_copy(j, k).wait_recv()
                    summed = summed + r.head_in[k, :, cols].astype(F32)
                r.mine[:, cols] = summed
                r.quad_out[:, cols] = summed.astype(BF16)
            for m in (2, 3, 1):
                start(quad_copy(s, m))

        def half_copy(s):
            cols = first_of(s)
            return remote(
                r.half_out.at[:, cols], r.half_in.at[:, cols], r.half_send.at[s], r.half_recv.at[s], opposite
            )

        def over_halves(s):
            summed = r.mine[*quarter(s, me)]
            for m in range(1, 4):
                quad_copy(s, m).wait_recv()
                summed = summed + r.quad_in[m, :, first_of(s)].astype(F32)
            r.half_out[:, first_of(s)] = summed.astype(BF16)
            start(half_copy(s))

        def full_copy(s, m):
            there = r.full.at[*quarter(s, me)]
            return remote(
                there, there, r.full_send.at[s * 4 + m], r.full_recv.at[s * 4 + m], quad_targets[m]
            )

        def to_quad(s):
            half_copy(s).wait_recv()
            cols = first_of(s)
            summed = r.half_out[:, cols].astype(F32) + r.half_in[:, cols].astype(F32)
            r.full[*quarter(s, me)] = summed.astype(BF16)
            for m in (2, 3, 1):
                start(full_copy(s, m))

        def full_here(s):
            for m in range(1, 4):
                arrival(r.full.at[*quarter(s, quad[m])], r.full_recv.at[s * 4 + m], quad_targets[m])

        def back_pair(pair):
            def image_back(i, carry):
                attend_back(i, pair, r)
                return carry

            lax.fori_loop(0, images, image_back, 0)
            over_head(1 + pair, tn(r.first[...], r.dtriple[:, pair * width : (pair + 1) * width]))

        over_head(0, tn(r.mixed[...], r.dattn[...]))
        back_pair(0)
        back_pair(1)
        after_x(1)
        back_pair(2)
        over_quad(0)
        moment_loads = [
            pltpu.make_async_copy(src, r.kept.at[k, :, 0:piece], r.load.at[4 + k])
            for k, src in enumerate((r.up_m_hbm, r.up_v_hbm, r.down_m_hbm, r.down_v_hbm))
        ]
        for copy in moment_loads:
            copy.start()

        def first_back(i, carry):
            first_norm_back(i, r)
            return carry

        lax.fori_loop(0, images, first_back, 0)
        over_head(4, jnp.concatenate([tail_grads(UNITS, r), jnp.zeros((width, LANES), F32)], axis=1))
        over_quad(1)
        over_halves(0)
        gather_images(images, r.dres, r.wide, r.input_grad)
        over_quad(2)
        over_halves(1)

        for i in range(1, UNITS):
            arrival(block(r.arrived, i, slots), r.a_recv.at[i], targets[i])

        def combine_out(i, carry):
            rows = pl.ds(pl.multiple_of(i * ROWS, 16), ROWS)
            out = r.resid[rows, :]
            spots = r.pos[rows, :]
            gate = r.gates[rows, :]
            for e in range(UNITS):
                at = spots[:, e : e + 1]
                share = jnp.where(at >= 0.0, gate[:, e : e + 1], 0.0)
                place = jnp.where(slot == at, 1.0, 0.0).astype(BF16)
                out = out + share * nn(place, r.arrived[e * slots : (e + 1) * slots, :])
            r.dsecond[rows, :] = out
            return carry

        lax.fori_loop(0, images, combine_out, 0)
        over_halves(2)
        to_quad(0)
        to_quad(1)
        gather_images(images, r.dsecond, r.wide, r.output)
        to_quad(2)

        weights_sq, steps_sq, tally = [], [], []

        def count_in(weight, grad, first, second):
            step = adam_terms(weight, grad, first, second)[2]
            return total_of(weight), total_of(step)

        for copy in moment_loads:
            copy.wait()
        for p, weight in enumerate((r.up_w, r.down_w)):

            @pl.when(c != zh)
            def _(p=p):
                arrival(r.sum_recv.at[0, :, halves[p]], r.f_recv.at[p * 2], sibling)

            arrival(r.sum_recv.at[1, :, halves[p]], r.f_recv.at[p * 2 + 1], sibling)
            grad = r.sum_recv[0, :, halves[p]].astype(F32) + r.sum_recv[1, :, halves[p]].astype(F32)
            tally += count_in(weight[...], grad, r.kept[2 * p, :, 0:piece], r.kept[2 * p + 1, :, 0:piece])
        for copy in loads:
            copy.wait()

        def dense_grad(j):
            return r.full[:, order[j]].astype(F32)

        full_here(0)
        full_here(1)
        for weight, first, second, blocks_of in (
            (r.qkv_w, r.qkv_m, r.qkv_v, range(9)),
            (r.proj_w, r.proj_m, r.proj_v, range(9, 12)),
        ):
            sums_of = [jnp.zeros((1, 1), F32), jnp.zeros((1, 1), F32)]
            for n, j in enumerate(blocks_of):
                cols = slice(n * LANES, (n + 1) * LANES)
                both = count_in(weight[:, cols], dense_grad(j), first[:, cols], second[:, cols])
                sums_of = [a + b for a, b in zip(sums_of, both, strict=True)]
            weights_sq.append(sums_of[0])
            steps_sq.append(sums_of[1])
        full_here(2)
        r.square[...] = jnp.zeros_like(r.square)
        r.square[0:rows_dev, :] = dense_grad(12)
        turned = jnp.transpose(r.square[...])
        both = count_in(r.router_w[...], turned[0:UNITS, 0:rows_dev], r.router_m[...], r.router_v[...])
        weights_sq.append(both[0])
        steps_sq.append(both[1])
        step = adam_terms(r.norm_w[...], turned[UNITS : UNITS + 4, 0:rows_dev], r.norm_m[...], r.norm_v[...])[2]
        for k in range(4):
            weights_sq.append(total_of(r.norm_w[k : k + 1, :]))
            steps_sq.append(total_of(step[k : k + 1, :]))
        spot = lane_index(1, LANES)
        row = jnp.zeros((1, LANES), F32)
        for k, value in enumerate(weights_sq + steps_sq + tally):
            row = jnp.where(spot == k, value, row)
        r.tallies[pl.ds(pl.multiple_of(h * 8, 8), 8), :] = jnp.broadcast_to(row, (8, LANES))
        for k, target in enumerate(relations):
            start(
                remote(block(r.tallies, h, 8), block(r.tallies, h, 8), r.n_send.at[k], r.n_recv.at[h], target)
            )
        for q, target in zip(related, relations, strict=True):
            arrival(block(r.tallies, q, 8), r.n_recv.at[q], target)
        summed = r.tallies[0:8, :]
        for q in range(1, 4):
            summed = summed + r.tallies[q * 8 : (q + 1) * 8, :]
        r.norm_row[...] = jnp.sqrt(summed)

        for wait in pending:
            wait()

    dma = pltpu.SemaphoreType.DMA
    scratch = (
        ((width, wide_dense), BF16),
        ((4, width, piece), BF16),
        ((4, width, piece), BF16),
        ((width, piece), BF16),
        ((width, piece), BF16),
        ((LANES, LANES), F32),
        ((UNITS * slots, width), BF16),
        ((UNITS * 8, width), F32),
        ((UNITS * slots, width), BF16),
        ((UNITS * slots, width), BF16),
        ((UNITS * slots, width), BF16),
        ((UNITS * slots, width), BF16),
        ((UNITS * 8, width), F32),
        ((UNITS * 8, width), F32),
        ((UNITS * slots, width), BF16),
        ((UNITS * 8, width), F32),
        ((UNITS * slots, width), BF16),
        ((GROUP * slots, 4 * piece), BF16),
        ((GROUP * slots, 4 * piece), BF16),
        ((4, width, 2 * piece), F32),
        ((2, width, 2 * piece), BF16),
        ((2, width, 2 * piece), BF16),
        ((2, width, 2 * piece), BF16),
        ((total, width), F32),
        ((total, width), F32),
        ((8, width), F32),
        ((width, width), F32),
        ((rows_dev, wide_grads), F32),
        ((3, rows_dev, wide_grads), BF16),
        ((3, rows_dev, wide_grads), BF16),
        ((rows_dev, wide_grads), BF16),
        ((4, part, wide_grads // 2), BF16),
        ((part, wide_grads // 2), BF16),
        ((part, wide_grads // 2), BF16),
        ((4 * 8, LANES), F32),
        ((rows_dev, 3 * width), F32),
        ((rows_dev, 3 * width), F32),
        ((rows_dev, width), F32),
        ((rows_dev, width), F32),
    )
    semaphores = (
        [dma((n,)) for n in (3, 4, 2, 2, 4, 4, 4)]
        + [dma((UNITS,))] * 12
        + [dma((4,))] * 4
        + [dma((15,))] * 2
        + [dma((12,))] * 2
        + [dma((3,))] * 2
        + [dma((12,))] * 2
        + [dma((4,)), dma((4,)), dma((8,))]
    )
    anywhere = pl.BlockSpec(memory_space=pl.ANY)
    return pl.pallas_call(
        body,
        out_shape=structs(
            (
                ((count, width), BF16),
                ((count, width), BF16),
                ((2, width, 2 * piece), BF16),
                ((rows_dev, wide_grads), BF16),
                ((8, LANES), F32),
            )
        ),
        in_specs=[VMEM] * 3 + [SMEM] + [VMEM] * 10 + [anywhere] * 8,
        out_specs=(VMEM,) * 5,
        scratch_shapes=buffers(saved) + buffers(routing) + buffers(scratch) + semaphores,
        compiler_params=params(mib=62, collective_id=1, has_side_effects=True),
        name="core",
    )(tokens, dout, routes, capacity, *weights, *small_moments, *moments)


def paired_finish(output, input_grad, expert_sums, full, norm_row, state):
    rows_dev = state[0].shape[0]
    width, piece = state[12].shape

    def body(*refs):
        (made, made_grad, sums, dense, norms) = refs[:5]
        state_refs, outs = refs[5:23], refs[23:]
        outs[0][...] = made[...]
        outs[1][...] = made_grad[...]
        order = dense_order(width)
        row = norms[0:1, :]
        square = jnp.concatenate(
            [dense[:, order[12]].astype(F32), jnp.zeros((LANES - rows_dev, LANES), F32)], axis=0
        )
        turned = jnp.transpose(square)

        def trust(over, under):
            return learn_rate * (row[:, over : over + 1] / row[:, under : under + 1])

        def update(which, grad, scale, cols=slice(None)):
            weight, first, second = [ref[:, cols] for ref in state_refs[3 * which : 3 * which + 3]]
            new, copy, first_new, second_new = outs[2 + 4 * which : 6 + 4 * which]
            first_here, second_here, step = adam_terms(weight, grad, first, second)
            first_new[:, cols] = first_here
            second_new[:, cols] = second_here
            value = weight - scale * step
            new[:, cols] = value
            copy[:, cols] = value.astype(BF16)

        for which, at, over in ((0, 0, 0), (1, 9, 1)):
            for n in range(9 if which == 0 else 3):
                cols = slice(n * LANES, (n + 1) * LANES)
                update(which, dense[:, order[at + n]].astype(F32), trust(over, over + 7), cols)
        update(2, turned[0:UNITS, 0:rows_dev], trust(2, 9))
        scales = jnp.concatenate([trust(3 + k, 10 + k) for k in range(4)], axis=0)
        update(3, turned[UNITS : UNITS + 4, 0:rows_dev], scales)
        for p in range(2):
            cols = slice(p * piece, (p + 1) * piece)
            grad = sums[0, :, cols].astype(F32) + sums[1, :, cols].astype(F32)
            update(4 + p, grad, trust(14 + 2 * p, 15 + 2 * p))
        dense_norms, expert_norms = outs[26:]
        dense_norms[0:1, :] = row[:, 0:7]
        dense_norms[1:2, :] = pltpu.roll(row, LANES - 7, 1)[:, 0:7]
        expert_norms[...] = pltpu.roll(row, LANES - 14, 1)[:, 0:4]

    results = []
    for k in range(0, len(state), 3):
        size = state[k].shape
        results += [(size, F32), (size, BF16), (size, F32), (size, F32)]
    return pl.pallas_call(
        body,
        out_shape=structs(
            [(output.shape, BF16), (input_grad.shape, BF16)] + results + [((2, 7), F32), ((1, 4), F32)]
        ),
        in_specs=[VMEM] * 23,
        out_specs=(VMEM,) * 28,
        compiler_params=params(),
        name="finish",
    )(output, input_grad, expert_sums, full, norm_row, *state)


def paired_step(
    block_input, out_cotangent, route_ids, capacity,
    qkv_weight, qkv_first, qkv_second,
    proj_weight, proj_first, proj_second,
    router_weight, router_first, router_second,
    norm_params, norm_first, norm_second,
    expert_up, up_first, up_second,
    expert_down, down_first, down_second,
):
    count = block_input.shape[0]
    slots = ceil_to(max(2, 3 * count // lax.axis_size("expert")), 16)
    state = (
        qkv_weight, qkv_first, qkv_second,
        proj_weight, proj_first, proj_second,
        router_weight.T, router_first.T, router_second.T,
        norm_params.T, norm_first.T, norm_second.T,
        expert_up[0], up_first[0], up_second[0],
        expert_down[0], down_first[0], down_second[0],
    )
    made = paired_core(
        block_input, out_cotangent, route_ids.T, capacity,
        state[0::3], (state[7], state[8], state[10], state[11]),
        (state[1], state[2], state[4], state[5], state[13], state[14], state[16], state[17]), slots,
    )
    block_output, input_grad, *results, dense_norms, expert_norms = paired_finish(*made, state)
    for k in range(8, 16):
        results[k] = results[k].T
    for k in range(16, 24):
        results[k] = results[k][None]
    return (block_output, input_grad, *results, dense_norms.T, expert_norms)


def solution(mesh):
    tokens, dense, pair = P(("expert", "head"), None), P("head", None), P("expert", None, "head")
    small = mesh.shape["expert"] == 8 and mesh.shape["head"] == 4
    return jax.shard_map(
        paired_step if small else plain_step,
        mesh=mesh,
        in_specs=(tokens,) * 3 + (P(),) + (dense,) * 12 + (pair,) * 6,
        out_specs=(tokens,) * 2 + (dense,) * 16 + (pair,) * 8 + (P(), P("expert", None)),
        check_vma=False,
    )
```

time: 541 us -> 154 us (0.28)
  waiting for transfers between devices: 267 us -> 0 us
  blocking collectives: 94.2 us -> 0 us
  Pallas kernels: 80.9 us -> 153 us
  other arithmetic: 40.6 us -> 0 us
  local copies, waits for them, and re-layouts: 31 us -> 0 us
  between operations: 18.9 us -> 0.85 us
  starting transfers between devices: 5.94 us -> 0 us
    reduce_scatter x3 -> x0, waiting for transfers between devices: 94.5 us -> none  [the longest x1 35.6 us: local(): lax.psum_scatter(grad_down, 'head', scatter_dimension=1, tiled=True)]
    all_to_all x1 -> x0, blocking collectives: 88 us -> none  [local(): lax.all_to_all(back.reshape(experts, slots, 2 * width), 'expert', split_a...]
    pallas_call x3 -> x2, Pallas kernels: 80.9 us -> 153 us  [the longest x1 144 us: paired_core(): pl.pallas_call(body, out_shape=structs((((count, width), BF16), ((count,...]
    psum x1 -> x0, waiting for transfers between devices: 70.7 us -> none  [local(): summed = lax.psum(summed, 'expert')]
    all_gather x3 -> x0, waiting for transfers between devices: 57.5 us -> none  [the longest x1 19.6 us: local(): lax.all_gather(expert_down[0].astype(BF16), 'head', axis=1, tiled=True)]
    all_to_all x1 -> x0, waiting for transfers between devices: 43.3 us -> none  [local(): lax.all_to_all(sent, 'expert', split_axis=0, concat_axis=0, tiled=True)]
    reduce_sum x8 -> x0, other arithmetic: 15.9 us -> none  [the longest x6 14.4 us: squares(): return jnp.sum(values * values)]
    unnamed x60 -> x0, local copies, waits for them, and re-layouts: 15.3 us -> none
  transfers between devices with their start and end apart: 8 -> 0, of which waited for: 8 -> 0; matrix products, arithmetic and copies ran while one was open for 3% -> 0% of each run, Pallas kernels for 0% -> 0%
where the time goes in v2:
time: 154 us
  Pallas kernels  153 us (99%)
    pallas_call x1, Pallas kernels, paired_core(): pl.pallas_call(body, out_shape=structs((((count, width), BF16), ((count,...  144 us
    pallas_call x1, Pallas kernels, paired_finish(): pl.pallas_call(body, out_shape=structs([(output.shape, BF16), (input_grad...  8.34 us

profile of v2, /device:TPU:0, one launch (start us, length us, event | category | flops | bytes accessed | tf_op | source)
XLA Modules:
  0.0 153.7 jit_solution(13947640753713523899)
XLA Ops:
  0.7 144.5 %core.1 = (bf16[788,384]{1,0:T(8,128)(2,1)}, bf16[788,384]{1,0:T(8,128)(2,1)}, bf16[2,384,768]{2,1,0:T(8,128)(2,1)}, bf16[96,1792]{1,0:T(8,128)(2,1)}, f32[8,128]{1,0:T(8,128)}) custom-call(bf16[788,384]{1,0:T(8,128)(2,1)} %refs_0_.1, bf16[788,384]{1,0:T(8,128)(2,1)} %refs_1_.1, s32[2,788]{1,0:T(2,128)} %bitcast.54, s32[8]{0:T(128)} %refs_3_.1, ...), custom_call_target="tpu_custom_call" | custom-call | tf_op jit(solution)/shard_map/core/pallas_call | solution.py:1465
  145.1 8.3 %finish.1 = (bf16[788,384]{1,0:T(8,128)(2,1)}, bf16[788,384]{1,0:T(8,128)(2,1)}, f32[96,1152]{1,0:T(8,128)}, bf16[96,1152]{1,0:T(8,128)(2,1)}, f32[96,1152]{1,0:...) custom-call(bf16[788,384]{1,0:T(8,128)(2,1)} %get-tuple-element.61.r, ...), custom_call_target="tpu_custom_call" | custom-call | tf_op jit(solution)/shard_map/finish/pallas_call | solution.py:1533
